TPU v7x, 32 devices: a whole 2x2x4 slice. The times are simulated.
32 devices in a mesh: seq: 8 (over z, y), ch: 4 (over x, core).
Axes of the slice: x: 2, y: 2, z: 4, core: 2. Of those that a mesh axis runs over, the one named last changes fastest.
Arguments:
- tokens: float32 [4, 2048, 2048], P(None, 'seq'), may hold values from -6 to 6
- cotangent: float32 [4, 2048, 2048], P(None, 'seq'), may hold values from -6 to 6
- doc_starts: int32 [4, 48], replicated, may hold values from 0 to 2047, as said below
- norm1_gain: float32 [2048], replicated, may hold values from 0.5 to 1.5
- branch_gate_w: float32 [2048, 2560], P('seq', 'ch'), may hold values from -0.125 to 0.125
- branch_in_w: float32 [2048, 2560], P('seq', 'ch'), may hold values from -0.125 to 0.125
- branch_out_w: float32 [2560, 2048], P('ch', 'seq'), may hold values from -0.25 to 0.25
- conv_weight: float32 [4, 2560], P(None, 'ch'), may hold values from -3 to 3
- conv_bias: float32 [2560], P('ch'), may hold values from -3 to 3
- decay_param: float32 [2560], P('ch'), may hold values from 3 to 16
- recur_gate_w: float32 [16, 160, 160], P('ch'), may hold values from -0.5 to 0.5
- recur_gate_b: float32 [2560], P('ch'), may hold values from -4 to 4
- input_gate_w: float32 [16, 160, 160], P('ch'), may hold values from -0.5 to 0.5
- input_gate_b: float32 [2560], P('ch'), may hold values from -4 to 4
- norm2_gain: float32 [2048], replicated, may hold values from 0.5 to 1.5
- mlp_gate_w: float32 [2048, 6144], P('seq', 'ch'), may hold values from -0.125 to 0.125
- mlp_up_w: float32 [2048, 6144], P('seq', 'ch'), may hold values from -0.125 to 0.125
- mlp_down_w: float32 [6144, 2048], P('ch', 'seq'), may hold values from -0.15625 to 0.15625
Outputs:
- result: float32 [4, 2048, 2048], P(None, 'seq')
- block_states: float32 [4, 8, 2560], P(None, 'seq', 'ch')
- token_grad: float32 [4, 2048, 2048], P(None, 'seq')
- norm1_gain_grad: float32 [2048], replicated
- branch_gate_w_grad: float32 [2048, 2560], P('seq', 'ch')
- branch_in_w_grad: float32 [2048, 2560], P('seq', 'ch')
- branch_out_w_grad: float32 [2560, 2048], P('ch', 'seq')
- conv_weight_grad: float32 [4, 2560], P(None, 'ch')
- conv_bias_grad: float32 [2560], P('ch')
- decay_param_grad: float32 [2560], P('ch')
- recur_gate_w_grad: float32 [16, 160, 160], P('ch')
- recur_gate_b_grad: float32 [2560], P('ch')
- input_gate_w_grad: float32 [16, 160, 160], P('ch')
- input_gate_b_grad: float32 [2560], P('ch')
- norm2_gain_grad: float32 [2048], replicated
- mlp_gate_w_grad: float32 [2048, 6144], P('seq', 'ch')
- mlp_up_w_grad: float32 [2048, 6144], P('seq', 'ch')
- mlp_down_w_grad: float32 [6144, 2048], P('ch', 'seq')
Inputs may be any that keep to these rules, and one draw needn't show every extreme that they name: `doc_starts`: each row lists 48 positions in ascending order, repeats allowed, the first 0; a document begins at every listed position.
All inputs are finite; a program needn't handle non-finite values.
Results may differ from a plain program's by a relative error of at most 0.011.
Values may be sent and summed in bfloat16 or wider, within the bound.
No kernel may reach another device: no remote copies, remote signals or barrier semaphores. Data moves between devices by JAX's collectives and lax.ppermute only.
A program may use at most 320 MiB of HBM per device.

v0:
```python
import jax
import jax.numpy as jnp
from jax import lax
from jax.sharding import PartitionSpec as P


def passed_along(value, axis, steps):
    count = lax.axis_size(axis)
    first, last = (max(0, -steps), min(count, count - steps))
    return lax.ppermute(value, axis, [(source, source + steps) for source in range(first, last)])


def prefix(value, axis, join, neutral, backward):
    count, mine = (lax.axis_size(axis), lax.axis_index(axis))
    pieces = jax.tree.map(lambda part: lax.all_gather(part, axis), value)
    if backward:
        pieces = jax.tree.map(lambda part: part[::-1], pieces)
        mine = count - 1 - mine
    total = jax.tree.map(
        lambda part, zero: jnp.full_like(part, 0) + jnp.asarray(zero, part.dtype), value, neutral
    )

    def step(position, total):
        longer = join(total, jax.tree.map(lambda part: part[position], pieces))
        return jax.tree.map(lambda new, old: jnp.where(position < mine, new, old), longer, total)

    return lax.fori_loop(0, count - 1, step, total)


def rms_norm(values, gain):
    return values * lax.rsqrt(jnp.mean(values * values, axis=-1, keepdims=True) + 1e-06) * gain


def tap_masks(reset_ext, length):
    blocked = reset_ext[:, 3 : 3 + length]
    mask_list = []
    for shift_lag in (1, 2, 3):
        mask_list.append(jnp.where(blocked, 0.0, 1.0)[..., None])
        blocked = blocked | reset_ext[:, 3 - shift_lag : 3 - shift_lag + length]
    return mask_list


def gate_values(conv_values, recur_weight, recur_bias, input_weight, input_bias):
    row_count, length, channels = conv_values.shape
    grouped = conv_values.reshape(row_count, length, recur_weight.shape[0], recur_weight.shape[1])
    recur_pre = (
        jnp.einsum(
            "rtbi,bij->rtbj", grouped, recur_weight, precision=lax.Precision.HIGHEST
        ).reshape(row_count, length, channels)
        + recur_bias
    )
    input_pre = (
        jnp.einsum(
            "rtbi,bij->rtbj", grouped, input_weight, precision=lax.Precision.HIGHEST
        ).reshape(row_count, length, channels)
        + input_bias
    )
    return (jax.nn.sigmoid(recur_pre), jax.nn.sigmoid(input_pre))


def decay_terms(recur_gate, param, reset_here):
    log_decay = -8.0 * jax.nn.softplus(-param) * recur_gate
    decay_rate = jnp.where(reset_here[..., None], 0.0, jnp.exp(log_decay))
    factor = jnp.where(reset_here[..., None], 1.0, jnp.sqrt(-jnp.expm1(2.0 * log_decay)))
    return (decay_rate, factor)


def affine(earlier, later):
    return (earlier[0] * later[0], later[0] * earlier[1] + later[1])


def project(left, right):
    return jnp.einsum("rtd,df->rtf", left, right, preferred_element_type=jnp.float32)


def project_back(left, right):
    return jnp.einsum("rtf,df->rtd", left, right, preferred_element_type=jnp.float32)


def outer_sum(left, right):
    return jnp.einsum("rtd,rtf->df", left, right, preferred_element_type=jnp.float32)


def body(
    tokens,
    cotangent,
    doc_starts,
    norm1_gain,
    branch_gate_w,
    branch_in_w,
    branch_out_w,
    conv_weight,
    conv_bias,
    decay_param,
    recur_gate_w,
    recur_gate_b,
    input_gate_w,
    input_gate_b,
    norm2_gain,
    mlp_gate_w,
    mlp_up_w,
    mlp_down_w,
):
    row_count, span_len = (tokens.shape[0], tokens.shape[1])
    seq_index = lax.axis_index("seq")
    positions = seq_index * span_len - 3 + jnp.arange(span_len + 3, dtype=jnp.int32)
    reset_ext = jnp.any(doc_starts[:, :, None] == positions[None, None, :], axis=1)
    reset_here = reset_ext[:, 3:]
    valid_list = tap_masks(reset_ext, span_len)
    low_gate = branch_gate_w.astype(jnp.bfloat16)
    low_input = branch_in_w.astype(jnp.bfloat16)
    low_output = branch_out_w.astype(jnp.bfloat16)
    low_mlp_gate = mlp_gate_w.astype(jnp.bfloat16)
    low_mlp_up = mlp_up_w.astype(jnp.bfloat16)
    low_mlp_down = mlp_down_w.astype(jnp.bfloat16)
    gate_full, input_full, output_full, mlpg_full, up_full, down_full = (
        lax.all_gather(low_gate, "seq", axis=0, tiled=True),
        lax.all_gather(low_input, "seq", axis=0, tiled=True),
        lax.all_gather(low_output, "seq", axis=1, tiled=True),
        lax.all_gather(low_mlp_gate, "seq", axis=0, tiled=True),
        lax.all_gather(low_mlp_up, "seq", axis=0, tiled=True),
        lax.all_gather(low_mlp_down, "seq", axis=1, tiled=True),
    )
    normed_one, norm_one_back = jax.vjp(rms_norm, tokens, norm1_gain)
    hidden_one = normed_one.astype(jnp.bfloat16)
    pre_gate = project(hidden_one, gate_full)
    pre_input = project(hidden_one, input_full)
    gate_act, gelu_back_one = jax.vjp(jax.nn.gelu, pre_gate)
    before = passed_along(pre_input[:, -3:, :], "seq", 1)
    extended = jnp.concatenate([before, pre_input], axis=1)
    lagged = [extended[:, 3 - shift_lag : 3 - shift_lag + span_len] for shift_lag in (1, 2, 3)]
    conv_out = conv_bias + conv_weight[0] * pre_input
    for shift_lag in (1, 2, 3):
        conv_out = (
            conv_out + conv_weight[shift_lag] * lagged[shift_lag - 1] * valid_list[shift_lag - 1]
        )
    (recur_gate, input_gate), gates_back = jax.vjp(
        gate_values, conv_out, recur_gate_w, recur_gate_b, input_gate_w, input_gate_b
    )

    def decay_local(gate_value, param):
        return decay_terms(gate_value, param, reset_here)

    (decay_rate, factor), decay_back = jax.vjp(decay_local, recur_gate, decay_param)
    driven = factor * input_gate * conv_out
    local_decay, local_state = lax.associative_scan(affine, (decay_rate, driven), axis=1)
    end_decay = local_decay[:, -1]
    end_state = local_state[:, -1]
    carry_state = prefix(
        (end_decay, end_state),
        "seq",
        affine,
        (jnp.ones_like(end_decay), jnp.zeros_like(end_state)),
        False,
    )[1]
    rec_state = local_state + local_decay * carry_state[:, None, :]
    block_states = rec_state[:, -1:, :]
    mixed_val = (gate_act * rec_state).astype(jnp.bfloat16)
    branch_out = lax.psum(project(mixed_val, output_full), "ch")
    after_one = tokens + branch_out
    normed_two, norm_two_back = jax.vjp(rms_norm, after_one, norm2_gain)
    hidden_two = normed_two.astype(jnp.bfloat16)
    pre_mlp = project(hidden_two, mlpg_full)
    pre_up = project(hidden_two, up_full)
    mlp_act, gelu_back_two = jax.vjp(jax.nn.gelu, pre_mlp)
    product = (mlp_act * pre_up).astype(jnp.bfloat16)
    mlp_out = lax.psum(project(product, down_full), "ch")
    result = after_one + mlp_out
    gate_back, input_back, output_back, mlpg_back, up_back, down_back = (
        lax.all_gather(low_gate, "seq", axis=0, tiled=True),
        lax.all_gather(low_input, "seq", axis=0, tiled=True),
        lax.all_gather(low_output, "seq", axis=1, tiled=True),
        lax.all_gather(low_mlp_gate, "seq", axis=0, tiled=True),
        lax.all_gather(low_mlp_up, "seq", axis=0, tiled=True),
        lax.all_gather(low_mlp_down, "seq", axis=1, tiled=True),
    )
    grad_two = cotangent.astype(jnp.bfloat16)
    grad_product = project_back(grad_two, down_back)
    grad_down = outer_sum(product, grad_two)
    grad_up = (grad_product * mlp_act).astype(jnp.bfloat16)
    grad_mlp = gelu_back_two(grad_product * pre_up)[0].astype(jnp.bfloat16)
    grad_mlpg_w = outer_sum(hidden_two, grad_mlp)
    grad_up_w = outer_sum(hidden_two, grad_up)
    grad_hidden_two = lax.psum(
        project_back(grad_mlp, mlpg_back) + project_back(grad_up, up_back), "ch"
    )
    grad_after_norm, grad_norm_two = norm_two_back(grad_hidden_two)
    grad_after = cotangent + grad_after_norm
    grad_one = grad_after.astype(jnp.bfloat16)
    grad_mixed = project_back(grad_one, output_back)
    grad_output_w = outer_sum(mixed_val, grad_one)
    grad_pre_gate = gelu_back_one(grad_mixed * rec_state)[0].astype(jnp.bfloat16)
    grad_direct = grad_mixed * gate_act
    next_decay = jnp.concatenate([decay_rate[:, 1:], jnp.ones_like(decay_rate[:, :1])], axis=1)
    tail_decay, local_grad = lax.associative_scan(
        affine, (next_decay, grad_direct), axis=1, reverse=True
    )
    export_alpha = decay_rate[:, 0] * tail_decay[:, 0]
    export_beta = decay_rate[:, 0] * local_grad[:, 0]
    incoming_grad = prefix(
        (export_alpha, export_beta),
        "seq",
        affine,
        (jnp.ones_like(export_alpha), jnp.zeros_like(export_beta)),
        True,
    )[1]
    grad_state = local_grad + tail_decay * incoming_grad[:, None, :]
    prior_state = jnp.concatenate([carry_state[:, None, :], rec_state[:, :-1]], axis=1)
    grad_decay = grad_state * prior_state
    grad_factor = grad_state * input_gate * conv_out
    grad_input_gate = grad_state * factor * conv_out
    grad_conv = grad_state * factor * input_gate
    grad_recur, grad_decay_param = decay_back((grad_decay, grad_factor))
    grad_conv_gates, grad_recur_w, grad_recur_b, grad_input_w, grad_input_b = gates_back(
        (grad_recur, grad_input_gate)
    )
    grad_conv = grad_conv + grad_conv_gates
    grad_conv_b = jnp.sum(grad_conv, axis=(0, 1))
    grad_conv_w = jnp.stack(
        [jnp.sum(grad_conv * pre_input, axis=(0, 1))]
        + [
            jnp.sum(grad_conv * valid_list[shift_lag - 1] * lagged[shift_lag - 1], axis=(0, 1))
            for shift_lag in (1, 2, 3)
        ],
        axis=0,
    )
    masked = [grad_conv * valid_list[shift_lag - 1] for shift_lag in (1, 2, 3)]
    outgoing = jnp.stack([piece[:, :3] for piece in masked], axis=0)
    incoming = passed_along(outgoing, "seq", -1)
    grad_input_sum = conv_weight[0] * grad_conv
    for shift_lag in (1, 2, 3):
        longer = jnp.concatenate([masked[shift_lag - 1], incoming[shift_lag - 1]], axis=1)
        grad_input_sum = (
            grad_input_sum + conv_weight[shift_lag] * longer[:, shift_lag : shift_lag + span_len]
        )
    grad_pre_input = grad_input_sum.astype(jnp.bfloat16)
    grad_gate_w = outer_sum(hidden_one, grad_pre_gate)
    grad_input_w_big = outer_sum(hidden_one, grad_pre_input)
    grad_hidden_one = lax.psum(
        project_back(grad_pre_gate, gate_back) + project_back(grad_pre_input, input_back), "ch"
    )
    grad_tokens_norm, grad_norm_one = norm_one_back(grad_hidden_one)
    token_grad = grad_after + grad_tokens_norm
    sum_gate, sum_input, sum_output, sum_mlpg, sum_up, sum_down = (
        lax.psum_scatter(grad_gate_w, "seq", scatter_dimension=0, tiled=True),
        lax.psum_scatter(grad_input_w_big, "seq", scatter_dimension=0, tiled=True),
        lax.psum_scatter(grad_output_w, "seq", scatter_dimension=1, tiled=True),
        lax.psum_scatter(grad_mlpg_w, "seq", scatter_dimension=0, tiled=True),
        lax.psum_scatter(grad_up_w, "seq", scatter_dimension=0, tiled=True),
        lax.psum_scatter(grad_down, "seq", scatter_dimension=1, tiled=True),
    )
    (
        sum_norm_one,
        sum_norm_two,
        sum_conv_w,
        sum_conv_b,
        sum_decay,
        sum_recur_w,
        sum_recur_b,
        sum_input_w,
        sum_input_b,
    ) = lax.psum(
        (
            grad_norm_one,
            grad_norm_two,
            grad_conv_w,
            grad_conv_b,
            grad_decay_param,
            grad_recur_w,
            grad_recur_b,
            grad_input_w,
            grad_input_b,
        ),
        "seq",
    )
    return (
        result,
        block_states,
        token_grad,
        sum_norm_one,
        sum_gate,
        sum_input,
        sum_output,
        sum_conv_w,
        sum_conv_b,
        sum_decay,
        sum_recur_w,
        sum_recur_b,
        sum_input_w,
        sum_input_b,
        sum_norm_two,
        sum_mlpg,
        sum_up,
        sum_down,
    )


def solution(mesh):
    in_specs = (
        P(None, "seq", None),
        P(None, "seq", None),
        P(),
        P(),
        P("seq", "ch"),
        P("seq", "ch"),
        P("ch", "seq"),
        P(None, "ch"),
        P("ch"),
        P("ch"),
        P("ch", None, None),
        P("ch"),
        P("ch", None, None),
        P("ch"),
        P(),
        P("seq", "ch"),
        P("seq", "ch"),
        P("ch", "seq"),
    )
    out_specs = (
        P(None, "seq", None),
        P(None, "seq", "ch"),
        P(None, "seq", None),
        P(),
        P("seq", "ch"),
        P("seq", "ch"),
        P("ch", "seq"),
        P(None, "ch"),
        P("ch"),
        P("ch"),
        P("ch", None, None),
        P("ch"),
        P("ch", None, None),
        P("ch"),
        P(),
        P("seq", "ch"),
        P("seq", "ch"),
        P("ch", "seq"),
    )
    return jax.shard_map(body, mesh=mesh, in_specs=in_specs, out_specs=out_specs, check_vma=False)
```

profile of v0, /device:TPU:0, one launch (start us, length us, event | category | flops | bytes accessed | tf_op | source)
XLA Modules:
  0.0 2893.4 jit_solution(13320221828569889540)
XLA Ops:
  23.1 45.1 %all-gather.13.cloned.1.call-done = bf16[2048,640]{1,0:T(8,128)(2,1)} async-done(((bf16[256,640]{1,0:T(8,128)(2,1)}), bf16[2048,640]{1,0:T(8,128)(2,1)}) %all-gather.13.cloned.1.call-update) | async-done | bytes 2621456 | tf_op jit(solution)/shard_map/all_gather | solution.py:118
  352.9 31.5 %all-gather.1 = f32[32,1,640]{2,1,0:T(1,128)S(1)} all-gather(f32[4,1,640]{2,1,0:T(1,128)S(1)} %slice_add_fusion.2), channel_id=3, replica_groups=mesh['seq'=8,'ch'=4] {'seq'}, dimensions={0}, use_global_device_ids=true | all-gather | bytes 92160 | tf_op jit(solution)/shard_map/all_gather | solution.py:15
  398.7 30.5 %all-gather = f32[32,1,640]{2,1,0:T(1,128)S(1)} all-gather(f32[4,1,640]{2,1,0:T(1,128)S(1)} %slice_add_fusion.3), channel_id=2, replica_groups=mesh['seq'=8,'ch'=4] {'seq'}, dimensions={0}, use_global_device_ids=true | all-gather | bytes 92160 | tf_op jit(solution)/shard_map/all_gather | solution.py:15
  429.8 12.8 multiply_convert_fusion.4
  459.0 144.6 %all-reduce.74.cloned.1.call-done = f32[4,256,2048]{2,1,0:T(8,128)} async-done(((f32[4,256,2048]{2,1,0:T(8,128)}), f32[4,256,2048]{2,1,0:T(8,128)}) %all-reduce.74.cloned.1.call-update) | async-done | bytes 8388624 | tf_op jit(solution)/shard_map/psum | solution.py:159
  620.3 85.1 %all-gather.19.cloned.1.call-done = bf16[2048,1536]{1,0:T(8,128)(2,1)} async-done(((bf16[256,1536]{1,0:T(8,128)(2,1)}), bf16[2048,1536]{1,0:T(8,128)(2,1)}) %all-gather.19.cloned.1.call-update) | async-done | bytes 6291472 | tf_op jit(solution)/shard_map/all_gather | solution.py:121
  705.5 11.9 fusion.17
  717.4 88.7 %all-gather.21.cloned.1.call-done = bf16[1536,2048]{1,0:T(8,128)(2,1)} async-done(((bf16[1536,256]{1,0:T(8,128)(2,1)}), bf16[1536,2048]{1,0:T(8,128)(2,1)}) %all-gather.21.cloned.1.call-update) | async-done | bytes 6291472 | tf_op jit(solution)/shard_map/all_gather | solution.py:122
  806.1 12.9 fusion.11
  819.0 86.5 %all-gather.17.cloned.1.call-done = bf16[2048,1536]{1,0:T(8,128)(2,1)} async-done(((bf16[256,1536]{1,0:T(8,128)(2,1)}), bf16[2048,1536]{1,0:T(8,128)(2,1)}) %all-gather.17.cloned.1.call-update) | async-done | bytes 6291472 | tf_op jit(solution)/shard_map/all_gather | solution.py:120
  905.5 18.5 fusion.10
  1002.4 11.7 fusion.13
  1014.1 82.1 %all-reduce.76.cloned.1.call-done = f32[4,256,2048]{2,1,0:T(8,128)} async-done(((f32[4,256,2048]{2,1,0:T(8,128)}), f32[4,256,2048]{2,1,0:T(8,128)}) %all-reduce.76.cloned.1.call-update) | async-done | bytes 8388624 | tf_op jit(solution)/shard_map/psum | solution.py:184
  1111.3 12.0 fusion.82
  1406.3 30.6 %all-gather.2 = f32[32,1,640]{2,1,0:T(1,128)S(1)} all-gather(f32[4,1,640]{2,1,0:T(1,128)S(1)} %get-tuple-element.316), channel_id=4, replica_groups=mesh['seq'=8,'ch'=4] {'seq'}, dimensions={0}, use_global_device_ids=true | all-gather | bytes 92160 | tf_op jit(solution)/shard_map/all_gather | solution.py:15
  1437.1 30.5 %all-gather.3 = f32[32,1,640]{2,1,0:T(1,128)S(1)} all-gather(f32[4,1,640]{2,1,0:T(1,128)S(1)} %get-tuple-element.315), channel_id=5, replica_groups=mesh['seq'=8,'ch'=4] {'seq'}, dimensions={0}, use_global_device_ids=true | all-gather | bytes 92160 | tf_op jit(solution)/shard_map/all_gather | solution.py:15
  1468.2 13.0 rev.15
  1481.3 21.0 rev.14
  1590.5 12.5 convolution_bitcast_fusion.2
  1603.0 12.7 convolution_bitcast_fusion.1
  1616.0 13.5 convolution_bitcast_fusion
  1633.9 206.2 %all-reduce.80.cloned.1.call-done = (f32[4,256,2048]{2,1,0:T(8,128)}, f32[4,256,2048]{2,1,0:T(8,128)}) async-done(((f32[4,256,2048]{2,1,0:T(8,128)}, f32[4,256,2048]{2,1,0:T(8,128)}), (f32[4,256,2048]{2,1,0:T(8,128)}, f32[4,256,2048]{2,1,0:T(8,128)})) %all-reduce.80.cloned.1.call-update) | async-done | bytes 16777232 | tf_op jit(solution)/shard_map/psum | solution.py:167
  1840.1 11.9 add.591
  1859.0 38.3 %all-reduce.66 = (f32[2048]{0:T(1024)}, f32[4,640]{1,0:T(4,128)}, f32[640]{0:T(1024)}, f32[640]{0:T(1024)}, f32[640]{0:T(1024)}, /*index=5*/f32[640]{0:T(1024)}, f32[2048]{0:T(1024)}) all-reduce(f32[2048]{0:T(1024)S(1)} %get-tuple-element.246, f32[4,640]{1,0:T(4,128)S(1)} %pad_maximum_fusion.32, ...), channel_id=1, replica_groups=mesh['seq'=8,'ch'=4] {'seq'}, use_global_device_ids=true, to_apply=%region_14.15 | all-reduce | flops 9216 | bytes 73728 | tf_op jit(solution)/shard_map/psum | solution.py:262
  1897.4 12.8 fusion.3
  1910.1 18.3 all-reduce.78.cloned.1.call-done
  1928.4 106.8 %reduce-scatter.11.cloned.1.call-done = f32[640,256]{1,0:T(8,128)} async-done(((f32[640,2048]{1,0:T(8,128)}), f32[640,256]{1,0:T(8,128)}) %reduce-scatter.11.cloned.1.call-update) | async-done | bytes 655376 | tf_op jit(solution)/shard_map/reduce_scatter | solution.py:247
  2035.2 106.8 %reduce-scatter.7.cloned.1.call-done = f32[256,640]{1,0:T(8,128)} async-done(((f32[2048,640]{1,0:T(8,128)}), f32[256,640]{1,0:T(8,128)}) %reduce-scatter.7.cloned.1.call-update) | async-done | bytes 655376 | tf_op jit(solution)/shard_map/reduce_scatter | solution.py:245
  2142.0 106.9 %reduce-scatter.9.cloned.1.call-done = f32[256,640]{1,0:T(8,128)} async-done(((f32[2048,640]{1,0:T(8,128)}), f32[256,640]{1,0:T(8,128)}) %reduce-scatter.9.cloned.1.call-update) | async-done | bytes 655376 | tf_op jit(solution)/shard_map/reduce_scatter | solution.py:246
  2248.9 211.6 %reduce-scatter.13.cloned.1.call-done = f32[256,1536]{1,0:T(8,128)} async-done(((f32[2048,1536]{1,0:T(8,128)}), f32[256,1536]{1,0:T(8,128)}) %reduce-scatter.13.cloned.1.call-update) | async-done | bytes 1572880 | tf_op jit(solution)/shard_map/reduce_scatter | solution.py:248
  2460.4 210.9 %reduce-scatter.15.cloned.1.call-done = f32[256,1536]{1,0:T(8,128)} async-done(((f32[2048,1536]{1,0:T(8,128)}), f32[256,1536]{1,0:T(8,128)}) %reduce-scatter.15.cloned.1.call-update) | async-done | bytes 1572880 | tf_op jit(solution)/shard_map/reduce_scatter | solution.py:249
  2671.3 211.3 %reduce-scatter.17.cloned.1.call-done = f32[1536,256]{1,0:T(8,128)} async-done(((f32[1536,2048]{1,0:T(8,128)}), f32[1536,256]{1,0:T(8,128)}) %reduce-scatter.17.cloned.1.call-update) | async-done | bytes 1572880 | tf_op jit(solution)/shard_map/reduce_scatter | solution.py:250
  (601 shorter events, 828.5 us)
Async XLA Ops:
  7.2 76.9 %copy-start = (f32[4,160,160]{2,1,0:T(8,128)S(1)}, f32[4,160,160]{2,1,0:T(8,128)}, u32[]{:S(2)}) copy-start(f32[4,160,160]{2,1,0:T(8,128)} %param.32) | copy-start | bytes 1228804
  7.2 61.0 %all-gather.13.cloned.1.call-start = ((), (), s32[]{:S(2)}) async-start(), calls=%async_computation.7 | async-start | bytes 2949120 | tf_op jit(solution)/shard_map/all_gather | solution.py:118
  9.2 420.5 %all-gather.11.cloned.1.call-start = ((), (), s32[]{:S(2)}) async-start(), calls=%async_computation.6 | async-start | bytes 2949120 | tf_op jit(solution)/shard_map/all_gather | solution.py:117
  11.2 431.4 %all-gather.15.cloned.1.call-start = ((), (), s32[]{:S(2)}) async-start(), calls=%async_computation.8 | async-start | bytes 2949120 | tf_op jit(solution)/shard_map/all_gather | solution.py:119
  12.0 591.6 %all-reduce.74.cloned.1.call-start = ((), (), s32[]{:S(2)}) async-start(), calls=%async_computation.9 | async-start | bytes 16777216 | tf_op jit(solution)/shard_map/psum | solution.py:159
  16.9 61.9 %copy-start.86 = (f32[4,256]{1,0:T(4,128)}, f32[4,256]{1,0:T(4,128)S(1)}, u32[]{:S(2)}) copy-start(f32[4,256]{1,0:T(4,128)S(1)} %get-tuple-element.388) | copy-start | bytes 12292
  17.0 61.9 %copy-start.88 = (f32[4,256]{1,0:T(4,128)}, f32[4,256]{1,0:T(4,128)S(1)}, u32[]{:S(2)}) copy-start(f32[4,256]{1,0:T(4,128)S(1)} %get-tuple-element.389) | copy-start | bytes 12292
  17.0 61.9 %copy-start.90 = (f32[4,256]{1,0:T(4,128)}, f32[4,256]{1,0:T(4,128)S(1)}, u32[]{:S(2)}) copy-start(f32[4,256]{1,0:T(4,128)S(1)} %get-tuple-element.390) | copy-start | bytes 12292
  17.0 83.7 %copy-start.80 = (f32[640]{0:T(1024)}, f32[640]{0:T(1024)S(1)}, u32[]{:S(2)}) copy-start(f32[640]{0:T(1024)S(1)} %fusion.109) | copy-start | bytes 7684
  23.1 53.6 %copy-start.95 = (f32[4,640]{1,0:T(4,128)S(1)}, f32[4,640]{1,0:T(4,128)}, u32[]{:S(2)}) copy-start(f32[4,640]{1,0:T(4,128)} %param.29) | copy-start | bytes 30724
  23.1 55.7 %copy-start.98 = (f32[640]{0:T(1024)S(1)}, f32[640]{0:T(1024)}, u32[]{:S(2)}) copy-start(f32[640]{0:T(1024)} %param.30) | copy-start | bytes 7684
  74.2 4.6 collective-permute-start
  76.8 23.9 copy-start.96
  346.6 38.0 %copy-start.67 = (f32[4,1,640]{2,1,0:T(1,128)S(1)}, f32[4,1,640]{2,1,0:T(1,128)}, u32[]{:S(2)}) copy-start(f32[4,1,640]{2,1,0:T(1,128)} %slice.782) | copy-start | bytes 30724
  451.5 254.0 %all-gather.19.cloned.1.call-start = ((), (), s32[]{:S(2)}) async-start(), calls=%async_computation.11 | async-start | bytes 7077888 | tf_op jit(solution)/shard_map/all_gather | solution.py:121
  454.0 352.1 %all-gather.21.cloned.1.call-start = ((), (), s32[]{:S(2)}) async-start(), calls=%async_computation.12 | async-start | bytes 7077888 | tf_op jit(solution)/shard_map/all_gather | solution.py:122
  456.4 449.1 %all-gather.17.cloned.1.call-start = ((), (), s32[]{:S(2)}) async-start(), calls=%async_computation.10 | async-start | bytes 7077888 | tf_op jit(solution)/shard_map/all_gather | solution.py:120
  459.0 154.8 %copy-start.47 = (f32[2048]{0:T(1024)S(1)}, f32[2048]{0:T(1024)}, u32[]{:S(2)}) copy-start(f32[2048]{0:T(1024)} %param.36) | copy-start | bytes 24580
  459.0 637.2 %all-reduce.76.cloned.1.call-start = ((), (), s32[]{:S(2)}) async-start(), calls=%async_computation.13 | async-start | bytes 16777216 | tf_op jit(solution)/shard_map/psum | solution.py:184
  945.0 895.1 %all-reduce.80.cloned.1.call-start = ((), (), s32[]{:S(2)}) async-start(), calls=%async_computation.21 | async-start | bytes 33554432 | tf_op jit(solution)/shard_map/psum | solution.py:167
  1239.2 21.2 copy-start.41
  1259.1 21.6 copy-start.62
  1404.5 63.7 %copy-start.20 = (f32[4,256,640]{2,1,0:T(8,128)S(1)}, f32[4,256,640]{2,1,0:T(8,128)}, u32[]{:S(2)}) copy-start(f32[4,256,640]{2,1,0:T(8,128)} %add.624) | copy-start | bytes 7864324
  1536.5 6.8 collective-permute-start.1
  1551.5 376.9 %all-reduce.78.cloned.1.call-start = ((), (), s32[]{:S(2)}) async-start(), calls=%async_computation.20 | async-start | bytes 2621440 | tf_op jit(solution)/shard_map/psum | solution.py:262
  1561.9 473.3 %reduce-scatter.11.cloned.1.call-start = ((), (), s32[]{:S(2)}) async-start(), calls=%async_computation.16 | async-start | bytes 5898240 | tf_op jit(solution)/shard_map/reduce_scatter | solution.py:247
  1571.5 570.5 %reduce-scatter.7.cloned.1.call-start = ((), (), s32[]{:S(2)}) async-start(), calls=%async_computation.14 | async-start | bytes 5898240 | tf_op jit(solution)/shard_map/reduce_scatter | solution.py:245
  1580.8 668.0 %reduce-scatter.9.cloned.1.call-start = ((), (), s32[]{:S(2)}) async-start(), calls=%async_computation.15 | async-start | bytes 5898240 | tf_op jit(solution)/shard_map/reduce_scatter | solution.py:246
  1590.3 870.1 %reduce-scatter.13.cloned.1.call-start = ((), (), s32[]{:S(2)}) async-start(), calls=%async_computation.17 | async-start | bytes 14155776 | tf_op jit(solution)/shard_map/reduce_scatter | solution.py:248
  1603.0 1068.3 %reduce-scatter.15.cloned.1.call-start = ((), (), s32[]{:S(2)}) async-start(), calls=%async_computation.18 | async-start | bytes 14155776 | tf_op jit(solution)/shard_map/reduce_scatter | solution.py:249
  1615.8 1266.9 %reduce-scatter.17.cloned.1.call-start = ((), (), s32[]{:S(2)}) async-start(), calls=%async_computation.19 | async-start | bytes 14155776 | tf_op jit(solution)/shard_map/reduce_scatter | solution.py:250
  1852.0 45.3 %copy-start.83 = (f32[4,256]{1,0:T(4,128)S(1)}, f32[4,256]{1,0:T(4,128)}, u32[]{:S(2)}) copy-start(f32[4,256]{1,0:T(4,128)} %copy-done.82) | copy-start | bytes 12292
  (91 other events, 674.6 us)
Sparse Core Ops, SparseCore 0:
  10.8 57.3 all-gather.12
  70.4 53.2 all-gather.10
  125.7 55.4 all-gather.14
  451.6 151.9 all-reduce.73
  606.3 99.1 all-gather.18
  708.0 98.1 all-gather.20
  808.3 97.1 all-gather.16
  945.1 151.0 all-reduce.75
  1551.6 288.4 all-reduce.79
  1844.2 84.1 all-reduce.77
  1933.0 102.1 reduce-scatter.10
  2039.6 102.3 reduce-scatter.6
  2146.5 102.2 reduce-scatter.8
  2253.3 207.0 reduce-scatter.12
  2464.8 206.4 reduce-scatter.14
  2675.8 206.8 reduce-scatter.16
where the time goes:
time: 2910 us; the launch traced here: 2890 us
  waiting for transfers between devices  1710 us (59%)
  local copies, waits for them, and re-layouts  537 us (18%)
  other arithmetic  249 us (9%)
  matrix products  210 us (7%)
  blocking collectives  162 us (6%)
    reduce_scatter x1, waiting for transfers between devices, body(): lax.psum_scatter(grad_mlpg_w, 'seq', scatter_dimension=0, tiled=True)  212 us
    reduce_scatter x1, waiting for transfers between devices, body(): lax.psum_scatter(grad_down, 'seq', scatter_dimension=1, tiled=True)  211 us
    reduce_scatter x1, waiting for transfers between devices, body(): lax.psum_scatter(grad_up_w, 'seq', scatter_dimension=0, tiled=True)  211 us
    psum x1, waiting for transfers between devices, body(): mlp_out = lax.psum(project(product, down_full), 'ch')  206 us
    slice x57, local copies, waits for them, and re-layouts, body(): lax.associative_scan(affine, (next_decay, grad_direct), axis=1, reverse=T...  183 us
    psum x1, waiting for transfers between devices, body(): branch_out = lax.psum(project(mixed_val, output_full), 'ch')  145 us
    all_gather x4, blocking collectives, prefix(): pieces = jax.tree.map(lambda part: lax.all_gather(part, axis), value)  123 us
    slice x52, local copies, waits for them, and re-layouts, body(): lax.associative_scan(affine, (decay_rate, driven), axis=1)  113 us
  transfers between devices with their start and end apart: 18, of which 16 were waited for; matrix products, arithmetic and copies ran while one was open for 19% of the time, Pallas kernels for 0%

commit v1 on v0

v1 whole, which is shorter than its diff:
```python
import jax
import jax.numpy as jnp
from jax import lax
from jax.experimental import pallas as pl
from jax.experimental.pallas import tpu as pltpu
from jax.sharding import PartitionSpec as P

LOW = jnp.bfloat16
F32 = jnp.float32
EPS = 1e-06
GELU_A = 0.7978845608028654
GELU_B = 0.044715
VMEM_LIMIT = 48 * 1024 * 1024
RING_LIMIT = 8
WINDOW = 256
SMALL_COST = pl.CostEstimate(flops=1, bytes_accessed=1, transcendentals=0)


def ring_order(count):
    return list(range(0, count, 2)) + list(range(count - 1, 0, -2))


def ring_place(seq_index, count):
    return jnp.where(seq_index % 2 == 0, seq_index // 2, count - 1 - seq_index // 2)


def ring_member(place, count):
    place = place % count
    return jnp.where(place < count // 2, 2 * place, 2 * (count - 1 - place) + 1)


def ring_pairs(count):
    order = ring_order(count)
    ahead = [(order[i], order[(i + 1) % count]) for i in range(count)]
    behind = [(target, source) for source, target in ahead]
    return ahead, behind


def ring_blocks(count):
    if count > RING_LIMIT:
        return [jnp.int32(0)]
    here = ring_place(lax.axis_index("seq"), count)
    offsets = [0]
    for step in range(1, count // 2):
        offsets += [-step, step]
    return [ring_member(here + offset, count) for offset in offsets + [count // 2]]


def ring_block(offset, count):
    if abs(offset) == count // 2:
        return count - 1
    return 2 * offset if offset >= 0 else -2 * offset - 1


def after_that(value, others):
    return lax.optimization_barrier((value, others))[0]


def meet(value, *rings):
    value, pieces = lax.optimization_barrier((value, [ring.latest for ring in rings]))
    for ring, came in zip(rings, pieces, strict=True):
        ring.replace(came)
    return value


class Gather:
    def __init__(self, shards, others=()):
        self.count = lax.axis_size("seq")
        self.shards = shards
        joined = jnp.concatenate(shards, axis=1) if len(shards) > 1 else shards[0]
        self.latest, self.others = (joined, joined), others
        self.up, self.down = [self.latest[0]], [self.latest[1]]

    def replace(self, pieces):
        self.latest = pieces
        if self.count <= RING_LIMIT:
            self.up[-1], self.down[-1] = pieces

    def step(self):
        if self.count <= RING_LIMIT and len(self.up) <= self.count // 2:
            ahead, behind = ring_pairs(self.count)
            cut = self.shards[0].shape[0] // 2
            first, second = self.latest
            if len(self.up) == self.count // 2:
                first, second = first[:cut], second[cut:]
            first, second = after_that((first, second), self.others)
            self.others = ()
            self.up.append(lax.ppermute(first, "seq", ahead))
            self.down.append(lax.ppermute(second, "seq", behind))
            self.latest = (self.up[-1], self.down[-1])
        return self.latest

    def full(self):
        if self.count > RING_LIMIT:
            return [lax.all_gather(shard, "seq", axis=0, tiled=True) for shard in self.shards]
        pieces = [self.up[0]]
        for first, second in zip(self.up[1:], self.down[1:], strict=True):
            pieces += [first, second]
        full, start = [], 0
        for shard in self.shards:
            stop = start + shard.shape[1]
            full.append(jnp.concatenate([piece[:, start:stop] for piece in pieces], axis=0))
            start = stop
        return full


class Reduce:
    def __init__(self, fulls, others=()):
        self.count = lax.axis_size("seq")
        self.fulls = fulls
        self.left = self.count // 2
        self.latest, self.sent = (), ()
        self.others = others

    def replace(self, pieces):
        self.latest = pieces

    def step(self):
        if self.count <= RING_LIMIT and self.left > 0:
            ahead, behind = ring_pairs(self.count)
            up, down = ring_step(self.fulls, self.latest, self.count, self.left)
            up, down = after_that((up, down), self.others)
            self.others = ()
            self.sent = (up, down)
            self.latest = (lax.ppermute(up, "seq", ahead), lax.ppermute(down, "seq", behind))
            self.left -= 1
        return self.sent

    def sums(self):
        if self.count > RING_LIMIT:
            return [
                lax.psum_scatter(full.astype(F32), "seq", scatter_dimension=0, tiled=True)
                for full in self.fulls
            ]
        return ring_step(self.fulls, self.latest, self.count, 0)


def ring_step(fulls, came, count, step):
    half, rows = count // 2, fulls[0].shape[0] // count
    widths = [full.shape[1] for full in fulls]
    total = sum(widths)
    parts = 4
    piece = rows // parts
    first, last = step == half, step == 0

    def kernel(*refs):
        ups, downs = refs[: len(fulls)], refs[len(fulls) : 2 * len(fulls)]
        rest = refs[2 * len(fulls) :]
        got, out = rest[: len(came)], rest[len(came) :]
        place = pl.program_id(0)
        start = 0
        for index, width in enumerate(widths):
            columns = slice(start, start + width)
            start += width
            up, down = ups[index][...].astype(F32), downs[index][...].astype(F32)
            if last:
                out[index][...] = up + got[0][:, columns].astype(F32) + got[1][:, columns].astype(F32)
                continue
            if not first:
                plus, minus = got[0][:, columns].astype(F32), got[1][:, columns].astype(F32)
                if step == half - 1:
                    plus = jnp.where(place < parts // 2, plus, 0.0)
                    minus = jnp.where(place >= parts // 2, minus, 0.0)
                up, down = up + plus, down + minus
            out[0][:, columns] = up.astype(LOW)
            out[1][:, columns] = down.astype(LOW)

    def at(place, offset=0):
        block = ring_block(place, count)
        return lambda i: (block * parts + i + offset, 0)

    grid = parts // 2 if first else parts
    blocks = [pl.BlockSpec((piece, w), at(step)) for w in widths]
    blocks += [pl.BlockSpec((piece, w), at(-step, parts // 2 if first else 0)) for w in widths]
    got_specs = [pl.BlockSpec((piece, total), lambda i: (i, 0))] * len(came)
    if step == half - 1:
        got_specs = [
            pl.BlockSpec((piece, total), lambda i: (jnp.minimum(i, parts // 2 - 1), 0)),
            pl.BlockSpec((piece, total), lambda i: (jnp.maximum(i - parts // 2, 0), 0)),
        ]
    if last:
        out_specs = [pl.BlockSpec((piece, w), lambda i: (i, 0)) for w in widths]
        out_shape = [shape_of((rows, w)) for w in widths]
    else:
        out_specs = [pl.BlockSpec((piece, total), lambda i: (i, 0))] * 2
        out_shape = [shape_of((grid * piece, total), LOW)] * 2
    return pl.pallas_call(
        kernel, grid=(grid,), in_specs=blocks + got_specs, out_specs=out_specs,
        out_shape=out_shape, compiler_params=params(), cost_estimate=SMALL_COST, name="ring_step",
    )(*fulls, *fulls, *came)


ROW_ORDER = (0, 2, 1, 3)


def near_pairs(count):
    return [(c, c ^ 1) for c in range(count)]


def far_pairs(count):
    return [(c, c ^ 2) for c in range(count)]


def to_near(value):
    return lax.ppermute(value, "ch", near_pairs(lax.axis_size("ch")))


def to_far(value):
    return lax.ppermute(value, "ch", far_pairs(lax.axis_size("ch")))


def spread_rows(own):
    far, near = to_far(own), to_near(own)
    return [own, far, near, to_near(far)]


def sum_over(value, axis, dtype=F32):
    count, step = lax.axis_size(axis), 1
    while step < count:
        sent = value.astype(dtype)
        came = lax.ppermute(sent, axis, [(c, c ^ step) for c in range(count)])
        value = sent.astype(F32) + came.astype(F32)
        step *= 2
    return value


def carried(ends, backward):
    count, mine = lax.axis_size("seq"), lax.axis_index("seq")
    pieces = to_all(ends[:, :2].reshape(-1, ends.shape[2]), "seq").reshape(
        count, ends.shape[0], 2, ends.shape[2]
    )
    total = jnp.zeros_like(ends[:, 0])
    for place in range(count - 1):
        member = count - 1 - place if backward else place
        counts = member > mine if backward else member < mine
        piece = pieces[member]
        total = jnp.where(counts, piece[:, 0] * total + piece[:, 1], total)
    return total


def to_all(value, axis):
    count = lax.axis_size(axis)
    return lax.all_to_all(
        jnp.broadcast_to(value[None], (count,) + value.shape), axis, 0, 0, tiled=True
    )


def row_block(shape, column=0):
    return pl.BlockSpec((1,) + shape, lambda row, *_: (row, 0, column))


def whole_block(shape):
    return pl.BlockSpec(shape, lambda row, *_: (0,) * len(shape))


def gelu_parts(value):
    tanh = jnp.tanh(GELU_A * (value + GELU_B * value * value * value))
    act = 0.5 * value * (1.0 + tanh)
    slope = 0.5 * (1.0 + tanh) + 0.5 * value * (1.0 - tanh * tanh) * GELU_A * (
        1.0 + 3.0 * GELU_B * value * value
    )
    return act, slope


def gelu(value):
    return gelu_parts(value)[0]


def minus_expm1(value):
    series = jnp.full_like(value, 1.0 / 11.0)
    for divisor in range(10, 1, -1):
        series = (1.0 + value * series) * (1.0 / divisor)
    series = -value * (1.0 + value * series)
    return jnp.where(value > -0.8, series, 1.0 - jnp.exp(value))


def split(value):
    high = value.astype(LOW)
    return high, (value - high.astype(F32)).astype(LOW)


def dot(left, right, contract):
    return lax.dot_general(left, right, (contract, ((), ())), preferred_element_type=F32)


def dot_three(left, right, contract):
    (left_high, left_low), (right_high, right_low) = left, right
    return (
        dot(left_high, right_high, contract)
        + dot(left_high, right_low, contract)
        + dot(left_low, right_high, contract)
    )


def windows(count, size):
    starts = [min(block * size // 128 * 128, count * size - WINDOW) for block in range(count)]
    return [(start, block * size - start) for block, start in enumerate(starts)]


def window_dots(value, high_ref, low_ref, first, spots, contract):
    parts = []
    for index, (start, _) in enumerate(spots):
        piece = split(value[:, start : start + WINDOW])
        weight = (high_ref[first + index], low_ref[first + index])
        parts.append((start, dot_three(piece, weight, contract)))
    columns = []
    for tile in range(0, value.shape[1], 128):
        total = None
        for start, part in parts:
            if start <= tile < start + WINDOW:
                share = part[:, tile - start : tile - start + 128]
                total = share if total is None else total + share
        columns.append(total)
    return jnp.concatenate(columns, axis=1)


def decay_and_factor(recur, coef, reset):
    log_decay = coef * recur
    plain = jnp.exp(log_decay)
    decay = jnp.where(reset, 0.0, plain)
    factor = jnp.where(reset, 1.0, jnp.sqrt(minus_expm1(2.0 * log_decay)))
    return plain, decay, factor


def tile_scan(alpha, beta, backward):
    place = lax.broadcasted_iota(jnp.int32, alpha.shape, 1)
    for step in (1, 2, 4):
        turn = 8 - step if backward else step
        inside = place < 8 - step if backward else place >= step
        other_alpha = pltpu.roll(alpha, turn, 1)
        other_beta = pltpu.roll(beta, turn, 1)
        beta = jnp.where(inside, alpha * other_beta + beta, beta)
        alpha = jnp.where(inside, alpha * other_alpha, alpha)
    return alpha, beta


def join_tiles(alpha_ref, beta_ref, backward):
    length, channels = alpha_ref.shape[1], alpha_ref.shape[2]
    groups = length // 8

    def step(index, carry):
        alpha_carry, beta_carry = carry
        group = groups - 1 - index if backward else index
        rows = pl.ds(pl.multiple_of(group * 8, 8), 8)
        alpha, beta = alpha_ref[0, rows, :], beta_ref[0, rows, :]
        beta = alpha * beta_carry + beta
        alpha = alpha * alpha_carry
        alpha_ref[0, rows, :] = alpha
        beta_ref[0, rows, :] = beta
        last = 0 if backward else 7
        return alpha[last : last + 1], beta[last : last + 1]

    start = (jnp.ones((1, channels), F32), jnp.zeros((1, channels), F32))
    return lax.fori_loop(0, groups, step, start, unroll=4)


def forward_kernel(
    input_ref, halo_ref, mask_ref, taps_ref, bias_ref, coef_ref, high_ref, low_ref, gate_bias_ref,
    conv_ref, recur_ref, gate_ref, alpha_ref, beta_ref, export_ref, extended,
):
    length, channels = input_ref.shape[1], input_ref.shape[2]
    extended[0:8, :] = halo_ref[0]
    extended[8 : 8 + length, :] = input_ref[0]
    masks = mask_ref[0]
    conv = bias_ref[...] + taps_ref[0:1, :] * input_ref[0]
    for lag in (1, 2, 3):
        lagged = extended[8 - lag : 8 - lag + length, :]
        conv = conv + taps_ref[lag : lag + 1, :] * lagged * masks[:, lag : lag + 1]
    conv_ref[0] = conv
    count = high_ref.shape[0] // 2
    spots = windows(count, channels // count)
    before = [
        window_dots(conv, high_ref, low_ref, first, spots, ((1,), (0,))) for first in (0, count)
    ]
    recur = jax.nn.sigmoid(before[0] + gate_bias_ref[:, :channels])
    gate = jax.nn.sigmoid(before[1] + gate_bias_ref[:, channels:])
    recur_ref[0] = recur
    gate_ref[0] = gate
    reset = masks[:, 0:1] > 0.5
    _, decay, factor = decay_and_factor(recur, coef_ref[...], reset)
    driven = factor * gate * conv
    grouped = (length // 8, 8, channels)
    alpha, beta = tile_scan(decay.reshape(grouped), driven.reshape(grouped), False)
    alpha_ref[0] = alpha.reshape(length, channels)
    beta_ref[0] = beta.reshape(length, channels)
    alpha, beta = join_tiles(alpha_ref, beta_ref, False)
    export_ref[0] = jnp.concatenate([alpha, beta, jnp.zeros((6, channels), F32)], axis=0)


def backscan_kernel(
    mixed_ref, pre_ref, state_ref, recur_ref, mask_ref, coef_ref,
    pre_grad_ref, alpha_ref, beta_ref, export_ref, extended,
):
    length, channels = mixed_ref.shape[1], mixed_ref.shape[2]
    act, slope = gelu_parts(pre_ref[0])
    mixed = mixed_ref[0]
    pre_grad_ref[0] = (mixed * state_ref[0] * slope).astype(LOW)
    reset = mask_ref[0][:, 0:1] > 0.5
    decay = jnp.where(reset, 0.0, jnp.exp(coef_ref[...] * recur_ref[0]))
    extended[0:length, :] = decay
    extended[length : length + 8, :] = jnp.ones((8, channels), F32)
    following = extended[1 : 1 + length, :]
    grouped = (length // 8, 8, channels)
    alpha, beta = tile_scan(following.reshape(grouped), (mixed * act).reshape(grouped), True)
    alpha_ref[0] = alpha.reshape(length, channels)
    beta_ref[0] = beta.reshape(length, channels)
    alpha, beta = join_tiles(alpha_ref, beta_ref, True)
    first = extended[0:1, :]
    export_ref[0] = jnp.concatenate(
        [first * alpha, first * beta, jnp.zeros((6, channels), F32)], axis=0
    )


def backward_kernel(
    alpha_ref, beta_ref, incoming_ref, state_ref, carry_ref, recur_ref, gate_ref, conv_ref,
    input_ref, halo_ref, mask_ref, taps_ref, coef_ref, high_ref, low_ref, pre_grad_ref,
    grad_ref, tail_ref, head_ref, weight_ref, sums_ref, extended, masked, weight_acc,
):
    length, channels = alpha_ref.shape[1], alpha_ref.shape[2]

    @pl.when(pl.program_id(0) == 0)
    def _():
        weight_acc[...] = jnp.zeros_like(weight_acc)
        sums_ref[...] = jnp.zeros_like(sums_ref)

    masks = mask_ref[0]
    reset = masks[:, 0:1] > 0.5
    recur, gate, conv, coef = recur_ref[0], gate_ref[0], conv_ref[0], coef_ref[...]
    plain, decay, factor = decay_and_factor(recur, coef, reset)
    grad = beta_ref[0] + alpha_ref[0] * incoming_ref[0]
    extended[0:8, :] = jnp.broadcast_to(carry_ref[0], (8, channels))
    extended[8 : 8 + length, :] = state_ref[0]
    prior = extended[7 : 7 + length, :]
    grad_decay = grad * prior
    grad_factor = grad * gate * conv
    grad_log = jnp.where(reset, 0.0, grad_decay * decay - grad_factor * plain * plain / factor)
    grad_recur = coef * grad_log * recur * (1.0 - recur)
    grad_gate = grad * factor * conv * gate * (1.0 - gate)
    count = high_ref.shape[0] // 2
    size = channels // count
    spots = windows(count, size)
    grad_conv = grad * factor * gate
    for first, values in ((0, grad_recur), (count, grad_gate)):
        for index, (start, _) in enumerate(spots):
            columns = slice(start, start + WINDOW)
            pair = split(conv[:, columns]), split(values[:, columns])
            weight_acc[first + index] += dot_three(*pair, ((0,), (0,)))
        grad_conv = grad_conv + window_dots(
            values, high_ref, low_ref, first, spots, ((1,), (1,))
        )

    @pl.when(pl.program_id(0) == pl.num_programs(0) - 1)
    def _():
        for index in range(2 * count):
            place = spots[index % count][1]
            turned = weight_acc[index]
            if place:
                turned = pltpu.roll(turned, WINDOW - place, 1)
            weight_ref[index] = turned[place : place + size].astype(LOW)


    def total(value):
        return jnp.sum(value, axis=0, keepdims=True)

    extended[0:8, :] = halo_ref[0]
    extended[8 : 8 + length, :] = input_ref[0]
    sums = [total(grad_conv), total(grad_conv * input_ref[0])]
    masked[0:8, :] = jnp.zeros((8, channels), F32)
    masked[8 + length : 16 + length, :] = jnp.zeros((8, channels), F32)
    spread = taps_ref[0:1, :] * grad_conv
    head = jnp.zeros((8, channels), F32)
    for lag in (1, 2, 3):
        kept = grad_conv * masks[:, lag : lag + 1]
        sums.append(total(kept * extended[8 - lag : 8 - lag + length, :]))
        masked[8 : 8 + length, :] = kept
        tap = taps_ref[lag : lag + 1, :]
        spread = spread + tap * masked[8 + lag : 8 + lag + length, :]
        head = head + tap * masked[lag : 8 + lag, :]
    sums += [total(recur * grad_log), total(grad_recur), total(grad_gate)]
    sums_ref[...] += jnp.concatenate(sums, axis=0)
    grad_ref[0, :, :channels] = spread.astype(LOW)
    grad_ref[0, :, channels:] = pre_grad_ref[0]
    tail_ref[0] = spread[length - 8 :, :]
    head_ref[0] = head


def params():
    return pltpu.CompilerParams(
        dimension_semantics=("arbitrary",), vmem_limit_bytes=VMEM_LIMIT
    )


def shape_of(shape, dtype=F32):
    return jax.ShapeDtypeStruct(shape, dtype)


def run_forward(pre, halo, masks, taps, bias, coef, high, low, gate_bias):
    rows, length, channels = pre.shape[0], pre.shape[1], taps.shape[1]
    block = row_block((length, channels))
    return pl.pallas_call(
        forward_kernel,
        grid=(rows,),
        in_specs=[
            block, row_block((8, channels)), row_block((length, 8)), whole_block((4, channels)),
            whole_block((1, channels)), whole_block((1, channels)), whole_block(high.shape),
            whole_block(low.shape), whole_block((1, 2 * channels)),
        ],
        out_specs=[block] * 5 + [row_block((8, channels))],
        out_shape=[shape_of((rows, length, channels))] * 5 + [shape_of((rows, 8, channels))],
        scratch_shapes=[pltpu.VMEM((length + 8, channels), F32)],
        compiler_params=params(), cost_estimate=SMALL_COST,
        name="forward_scan",
    )(pre, halo, masks, taps, bias, coef, high, low, gate_bias)


def run_backscan(mixed, pre, state, recur, masks, coef):
    rows, length, channels = mixed.shape
    block = row_block((length, channels))
    return pl.pallas_call(
        backscan_kernel,
        grid=(rows,),
        in_specs=[
            block, row_block((length, channels), 1), block, block, row_block((length, 8)),
            whole_block((1, channels)),
        ],
        out_specs=[block] * 3 + [row_block((8, channels))],
        out_shape=[
            shape_of(mixed.shape, LOW), shape_of(mixed.shape), shape_of(mixed.shape),
            shape_of((rows, 8, channels)),
        ],
        scratch_shapes=[pltpu.VMEM((length + 8, channels), F32)],
        compiler_params=params(), cost_estimate=SMALL_COST,
        name="backward_scan",
    )(mixed, pre, state, recur, masks, coef)


def run_backward(
    alpha, beta, incoming, state, carry, recur, gate, conv, pre, halo, masks, taps, coef, high, low, pre_grad
):
    rows, length, channels = alpha.shape
    block, edge, line = (
        row_block((length, channels)), row_block((8, channels)), row_block((1, channels)),
    )
    weights = (high.shape[0], 2 * channels // high.shape[0], WINDOW)
    return pl.pallas_call(
        backward_kernel,
        grid=(rows,),
        in_specs=[
            block, block, line, block, line, block, block, block, block, edge,
            row_block((length, 8)), whole_block((4, channels)), whole_block((1, channels)),
            whole_block(high.shape), whole_block(low.shape), block,
        ],
        out_specs=[row_block((length, 2 * channels)), edge, edge, whole_block(weights), whole_block((8, channels))],
        out_shape=[
            shape_of((rows, length, 2 * channels), LOW), shape_of((rows, 8, channels)),
            shape_of((rows, 8, channels)), shape_of(weights, LOW), shape_of((8, channels)),
        ],
        scratch_shapes=[
            pltpu.VMEM((length + 8, channels), F32), pltpu.VMEM((length + 16, channels), F32),
            pltpu.VMEM(high.shape, F32),
        ],
        compiler_params=params(), cost_estimate=SMALL_COST,
        name="branch_backward",
    )(alpha, beta, incoming, state, carry, recur, gate, conv, pre, halo, masks, taps, coef, high, low, pre_grad)


def back_project(lefts, rights):
    rows, length, _ = lefts[0].shape
    width, tile = rights[0].shape[0], 256
    half = rows // 2

    def kernel(*refs):
        total = None
        for left, right in zip(refs[: len(lefts)], refs[len(lefts) : 2 * len(lefts)], strict=True):
            flat = left[...].reshape(rows * length, left.shape[2])
            share = dot(flat, right[...], ((1,), (1,)))
            total = share if total is None else total + share
        total = total.reshape(rows, length, tile)
        refs[-2][...] = total[:half]
        refs[-1][...] = total[half:].astype(LOW)

    out = pl.BlockSpec((half, length, tile), lambda i: (0, 0, i))
    in_specs = [pl.BlockSpec(left.shape, lambda i: (0, 0, 0)) for left in lefts]
    in_specs += [pl.BlockSpec((tile, right.shape[1]), lambda i: (i, 0)) for right in rights]
    return pl.pallas_call(
        kernel, grid=(width // tile,), in_specs=in_specs, out_specs=[out, out],
        out_shape=[shape_of((half, length, width)), shape_of((half, length, width), LOW)],
        compiler_params=params(), cost_estimate=SMALL_COST, name="back_project",
    )(*lefts, *rights)


def joined(kept, came):
    total = kept + came.astype(F32)
    return total[0:1], total[1:2].astype(LOW)


def part(index, width):
    return pl.ds(pl.multiple_of(index * width, 128), width)


def norm_kernel(row_map, block_map, gain_ref, values_ref, out_ref):
    blocks = block_map.shape[0]
    width = values_ref.shape[2] // blocks
    values = values_ref[0]
    root = lax.rsqrt(jnp.mean(values * values, axis=-1, keepdims=True) + EPS)
    for place in range(blocks):
        there = part(block_map[place], width)
        normed = values_ref[0, :, there] * root * gain_ref[:, there]
        out_ref[0, :, place * width : (place + 1) * width] = normed.astype(LOW)


def relative_kernel(row_map, block_map, values_ref, own_ref, *out_refs):
    blocks = block_map.shape[0]
    width = values_ref.shape[2] // blocks
    for place in range(blocks):
        there = part(block_map[place], width)
        here = slice(place * width, (place + 1) * width)
        for out_ref in out_refs:
            out_ref[0, :, here] = values_ref[0, :, there].astype(LOW)

        @pl.when(pl.program_id(0) == 0)
        def _():
            own_ref[0, :, here] = values_ref[0, :, there]


def assemble_kernel(row_map, block_map, base_ref, *refs):
    pieces, out_ref = refs[:-1], refs[-1]
    blocks = block_map.shape[0]
    width = base_ref.shape[2] // blocks
    for row, piece in enumerate(pieces):

        @pl.when(pl.program_id(0) == row)
        def _():
            for place in range(blocks):
                there = part(block_map[place], width)
                here = slice(place * width, (place + 1) * width)
                out_ref[0, :, there] = base_ref[0, :, there] + piece[0, :, here].astype(F32)


def arranged(kernel, maps, out_shape, in_specs, out_specs, *arrays):
    return pl.pallas_call(
        kernel,
        grid_spec=pltpu.PrefetchScalarGridSpec(
            num_scalar_prefetch=2, grid=(maps[0].shape[0],), in_specs=in_specs, out_specs=out_specs
        ),
        out_shape=out_shape,
        compiler_params=params(), cost_estimate=SMALL_COST,
    )(*maps, *arrays)


def mapped_row(shape):
    return pl.BlockSpec((1,) + shape, lambda row, row_map, block_map: (row_map[row], 0, 0))


def relative_norm(values, gain, maps):
    shape = values.shape[1:]
    return arranged(
        norm_kernel, maps, shape_of(values.shape, LOW),
        [whole_block((1, shape[1])), mapped_row(shape)], row_block(shape), gain[None, :], values,
    )


def relative_rows(values, maps, rounded):
    shape = values.shape[1:]
    shapes, specs = [shape_of((1,) + shape)], [whole_block((1,) + shape)]
    if rounded:
        shapes, specs = shapes + [shape_of(values.shape, LOW)], specs + [row_block(shape)]
    if not rounded:
        maps = (maps[0][:1], maps[1])
    return arranged(relative_kernel, maps, shapes, [mapped_row(shape)], specs, values)


def assemble(base, pieces, maps):
    shape = base.shape[1:]
    return arranged(
        assemble_kernel, maps, shape_of(base.shape),
        [mapped_row(shape)] + [whole_block((1,) + shape)] * len(pieces), mapped_row(shape),
        base, *pieces,
    )


def project(left, right):
    return jnp.einsum("rtd,df->rtf", left, right, preferred_element_type=F32)


def project_back(left, right):
    return jnp.einsum("rtf,df->rtd", left, right, preferred_element_type=F32)


def outer_sum(left, right):
    return jnp.einsum("rtd,rtf->df", left, right, preferred_element_type=F32).astype(LOW)


def inverse_root(values):
    return lax.rsqrt(jnp.mean(values * values, axis=-1, keepdims=True) + EPS)


def norm_back(grad, values, root, gain):
    scaled = grad * gain
    inner = jnp.mean(scaled * values, axis=-1, keepdims=True)
    share = jnp.sum(grad * values * root, axis=(0, 1))
    return root * scaled - values * (root * root * root) * inner, share


def gate_matrix_kernel(recur_ref, input_ref, high_ref, low_ref):
    count, size = recur_ref.shape[0], recur_ref.shape[1]
    high_ref[...] = jnp.zeros_like(high_ref)
    low_ref[...] = jnp.zeros_like(low_ref)
    for index, ref in enumerate((recur_ref, input_ref)):
        for block, (_, place) in enumerate(windows(count, size)):
            high, low = split(ref[block])
            here = slice(place, place + size)
            high_ref[index * count + block, here, here] = high
            low_ref[index * count + block, here, here] = low


def gate_matrix(recur_weight, input_weight):
    shape = shape_of((2 * recur_weight.shape[0], WINDOW, WINDOW), LOW)
    return pl.pallas_call(
        gate_matrix_kernel, out_shape=[shape, shape],
        compiler_params=pltpu.CompilerParams(vmem_limit_bytes=VMEM_LIMIT), cost_estimate=SMALL_COST, name="gate_matrix",
    )(recur_weight, input_weight)


def body(
    tokens, cotangent, doc_starts, norm1_gain, branch_gate_w, branch_in_w, branch_out_w,
    conv_weight, conv_bias, decay_param, recur_gate_w, recur_gate_b, input_gate_w, input_gate_b,
    norm2_gain, mlp_gate_w, mlp_up_w, mlp_down_w,
):
    rows, length, width = tokens.shape
    channels, blocks = conv_bias.shape[0], recur_gate_w.shape[0]
    seq_count = lax.axis_size("seq")
    mine, turn = lax.axis_index("seq"), lax.axis_index("ch")
    row_map = jnp.stack([turn ^ row for row in ROW_ORDER]).astype(jnp.int32)
    block_map = jnp.stack(ring_blocks(seq_count)).astype(jnp.int32)
    maps = (row_map, block_map)

    def row_of(values, row):
        return lax.dynamic_slice_in_dim(values, turn ^ ROW_ORDER[row], 1, axis=0)

    def features(values):
        return jnp.take(values.reshape(block_map.shape[0], -1), block_map, axis=0).reshape(-1)

    def features_back(values):
        there = jnp.argmax(block_map[None, :] == jnp.arange(block_map.shape[0])[:, None], axis=1)
        return jnp.take(values.reshape(block_map.shape[0], -1), there, axis=0).reshape(-1)

    gather_one = Gather(
        [
            jnp.concatenate([branch_in_w.astype(LOW), branch_gate_w.astype(LOW)], axis=1),
            branch_out_w.astype(LOW).T,
        ]
    )
    came = gather_one.step()

    starts = jnp.concatenate([row_of(doc_starts, j) for j in range(rows)], axis=0)
    positions = mine * length - 3 + jnp.arange(length + 3, dtype=jnp.int32)
    reset_ext = jnp.any(starts[:, :, None] == positions[None, None, :], axis=1)
    blocked = reset_ext[:, 3:]
    columns = [blocked.astype(F32)]
    for lag in (1, 2, 3):
        columns.append(jnp.where(blocked, 0.0, 1.0))
        blocked = blocked | reset_ext[:, 3 - lag : 3 - lag + length]
    masks = jnp.stack(columns + [jnp.zeros_like(columns[0])] * 4, axis=-1)

    gate_bias = jnp.concatenate([recur_gate_b, input_gate_b])[None, :]
    coef = (-8.0 * jax.nn.softplus(-decay_param))[None, :]
    gain_one, gain_two = features(norm1_gain), features(norm2_gain)
    mlp_shards = [mlp_gate_w.astype(LOW), mlp_up_w.astype(LOW)]
    down_shards = [mlp_down_w.astype(LOW).T]

    before = after_that(tokens[:, -8:, :], came)
    before = lax.ppermute(before, "seq", [(s, s + 1) for s in range(seq_count - 1)])
    first_maps = after_that(maps, (came, masks))
    came = gather_one.step()
    hidden_one = relative_norm(tokens, norm1_gain, first_maps)
    hidden_before = relative_norm(before, norm1_gain, first_maps)
    recur_weights = after_that(recur_gate_w, (came, hidden_before))
    came = gather_one.step()
    high, low = gate_matrix(recur_weights, input_gate_w)
    gather_two = Gather(mlp_shards, gather_one.step())
    gather_two.step()
    in_gate, output_full = gather_one.full()

    pre = project(hidden_one, in_gate)
    halo = project(hidden_before, in_gate)
    conv, recur, gate, decay_sum, state_part, export = run_forward(
        pre, halo, masks, conv_weight, conv_bias[None, :], coef, high, low, gate_bias
    )
    export = meet(export, gather_two)
    carry = carried(export, False)[:, None, :]
    came = gather_two.step()
    state = state_part + decay_sum * carry
    mixed = (gelu(pre[:, :, channels:]) * state).astype(LOW)

    kept, away = back_project([mixed], [output_full])
    kept, beyond = joined(kept, to_near(away))
    arrived = to_far(beyond)
    late_maps = after_that(maps, beyond)
    (tokens_own,) = relative_rows(tokens, late_maps, False)
    cotangent_own, grad_two = relative_rows(cotangent, late_maps, True)
    kept = meet(after_that(kept, (tokens_own, cotangent_own)), gather_two)
    after = tokens_own + (kept + arrived.astype(F32))
    came = gather_two.step()
    root_two = inverse_root(after)
    spread = spread_rows((after * root_two * gain_two).astype(LOW))
    gather_three = Gather(down_shards, gather_two.step())
    came = gather_three.step()
    hidden_two = jnp.concatenate(spread, axis=0)
    mlp_gate_full, mlp_up_full = gather_two.full()
    pre_mlp = project(hidden_two, mlp_gate_full)
    mlp_up_full = after_that(mlp_up_full, (came, pre_mlp))
    came = gather_three.step()
    pre_up = project(hidden_two, mlp_up_full)
    product = (gelu(pre_mlp) * pre_up).astype(LOW)
    grad_two = after_that(grad_two, (came, product))
    came = gather_three.step()
    down_part = outer_sum(grad_two, product)
    reduce_down = Reduce([down_part], gather_three.step())
    (mlp_down_full,) = gather_three.full()

    sent = reduce_down.step()
    grad_product = project(grad_two, after_that(mlp_down_full, sent))
    act, slope = gelu_parts(pre_mlp)
    grad_up = (grad_product * act).astype(LOW)
    grad_mlp = meet((grad_product * pre_up * slope).astype(LOW), reduce_down)
    sent = reduce_down.step()

    kept, away = back_project([after_that(grad_mlp, sent), grad_up], [mlp_gate_full, mlp_up_full])
    away = meet(away, reduce_down)
    sent = reduce_down.step()
    came = to_near(away)
    mlp_gate_part = outer_sum(after_that(hidden_two, (sent, away)), grad_mlp)
    kept, beyond = joined(kept, after_that(came, mlp_gate_part))
    beyond = meet(beyond, reduce_down)
    sent = reduce_down.step()
    arrived = to_far(beyond)
    mlp_up_part = outer_sum(after_that(hidden_two, (sent, beyond)), grad_up)
    result_kept, result_away = back_project([after_that(product, mlp_up_part)], [mlp_down_full])
    arrived = meet(after_that(arrived, result_away), reduce_down)
    reduce_gate = Reduce([mlp_gate_part], reduce_down.latest)
    reduce_up = Reduce([mlp_up_part], reduce_down.latest)
    sent = (reduce_gate.step(), reduce_up.step())
    back_two, share_two = norm_back(kept + arrived.astype(F32), after, root_two, gain_two)
    grad_after = cotangent_own + back_two
    own = after_that(grad_after.astype(LOW), sent)
    far, near = to_far(own), to_near(own)
    result_came = to_near(after_that(result_away, own))
    (grad_down,) = reduce_down.sums()
    grad_down = meet(grad_down, reduce_gate, reduce_up)
    sent = (reduce_gate.step(), reduce_up.step())
    far = after_that(far, sent)
    grad_one = jnp.concatenate([own, far, near, to_near(far)], axis=0)

    grad_mixed = project(after_that(grad_one, sent), output_full)
    grad_pre_gate, tail_decay, grad_part, export = run_backscan(
        grad_mixed, pre, state, recur, masks, coef
    )
    export = meet(export, reduce_gate, reduce_up)
    sent = (reduce_gate.step(), reduce_up.step())
    result_kept, result_beyond = joined(result_kept, after_that(result_came, (export, sent)))
    result_arrived = to_far(result_beyond)
    incoming = after_that(carried(export, True), result_beyond)[:, None, :]
    grad_pre, tail, head, gate_grads, sums = run_backward(
        tail_decay, grad_part, incoming, state, carry, recur, gate, conv, pre, halo, masks,
        conv_weight, coef, high, low, grad_pre_gate,
    )
    head = meet(after_that(head, result_arrived), reduce_gate, reduce_up)
    sent = reduce_gate.step()
    beyond = lax.ppermute(head, "seq", [(s + 1, s) for s in range(seq_count - 1)])
    result_delta = after + (result_kept + after_that(result_arrived, (sent, head)).astype(F32))
    result_delta = (result_delta - tokens_own).astype(LOW)
    result_far, result_near = to_far(result_delta), to_near(result_delta)
    out_part = outer_sum(grad_one, after_that(mixed, result_delta))
    beyond = after_that(beyond, out_part)
    grad_pre = lax.dynamic_update_slice(grad_pre, (tail + beyond).astype(LOW), (0, length - 8, 0))
    kept, away = back_project([grad_pre], [in_gate])
    away = meet(away, reduce_gate)
    reduce_up.others = away
    sent = reduce_up.step()
    came = to_near(away)
    gate_part = outer_sum(after_that(hidden_one, sent), grad_pre_gate)
    sum_rows = sums.astype(LOW).reshape(-1, WINDOW)
    small = jnp.concatenate(
        [
            gate_grads.reshape(-1, WINDOW),
            jnp.pad(sum_rows, ((0, -sum_rows.shape[0] % seq_count), (0, 0))),
        ]
    )
    small = after_that(small.reshape(seq_count, -1, WINDOW), away)
    small = lax.all_to_all(small, "seq", 0, 0, tiled=True)
    small = jnp.sum(small.astype(F32), axis=0)
    kept, beyond = joined(kept, after_that(came, gate_part))
    arrived = to_far(beyond)
    every = to_all(after_that(small, beyond).astype(LOW), "seq")
    result_pieces = [result_delta, result_far, result_near, to_near(after_that(result_far, beyond))]

    in_part = outer_sum(after_that(hidden_one, beyond), grad_pre[:, :, :channels])
    in_part = meet(in_part, reduce_up)
    reduce_branch = Reduce([out_part, gate_part, in_part], reduce_up.latest)
    sent = reduce_branch.step()

    arrived = after_that(arrived, sent)
    back_one, share_one = norm_back(
        kept + arrived.astype(F32), tokens_own, inverse_root(tokens_own), gain_one
    )
    token_own = meet(grad_after + back_one, reduce_branch)
    sent = reduce_branch.step()
    own = (token_own - cotangent_own).astype(LOW)
    far, near = to_far(own), to_near(own)
    shares = jnp.stack([features_back(share_one), features_back(share_two)]).reshape(-1, WINDOW)
    every_share = to_all(after_that(shares, own), ("seq", "ch"))
    (grad_mlp_gate_w,) = reduce_gate.sums()
    (grad_mlp_up_w,) = reduce_up.sums()
    far = meet(after_that(far, (grad_mlp_gate_w, grad_mlp_up_w)), reduce_branch)
    sent = reduce_branch.step()
    late_maps = after_that(maps, (sent, far))
    token_grad = assemble(cotangent, [own, far, near, to_near(far)], late_maps)
    late_maps = after_that(maps, token_grad)
    result = assemble(tokens, result_pieces, late_maps)
    result = meet(result, reduce_branch)
    reduce_branch.step()
    every, every_share = after_that((every, every_share), result)
    every = every.astype(F32)
    grad_out_w, grad_gate_w, grad_in_w = reduce_branch.sums()
    norm_shares = jnp.sum(every_share, axis=0).reshape(2, width)
    every = every.reshape(-1, WINDOW)
    size = channels // blocks
    gate_w = every[: 2 * channels].reshape(2 * blocks, size, WINDOW)[:, :, :size]
    sums = every[2 * channels : 2 * channels + sum_rows.shape[0]].reshape(sums.shape)
    swapped = turn // 2 + turn % 2 * 2
    block_states = jnp.concatenate(
        [
            lax.dynamic_slice_in_dim(state[:, -1:, :], swapped ^ row, 1, axis=0)
            for row in ROW_ORDER
        ],
        axis=0,
    )
    return (
        result,
        block_states,
        token_grad,
        norm_shares[0],
        grad_gate_w,
        grad_in_w,
        grad_out_w.T,
        sums[1:5],
        sums[0],
        8.0 * jax.nn.sigmoid(-decay_param) * sums[5],
        gate_w[:blocks],
        sums[6],
        gate_w[blocks:],
        sums[7],
        norm_shares[1],
        grad_mlp_gate_w,
        grad_mlp_up_w,
        grad_down.T,
    )


def solution(mesh):
    in_specs = (
        P(None, "seq", None),
        P(None, "seq", None),
        P(),
        P(),
        P("seq", "ch"),
        P("seq", "ch"),
        P("ch", "seq"),
        P(None, "ch"),
        P("ch"),
        P("ch"),
        P("ch", None, None),
        P("ch"),
        P("ch", None, None),
        P("ch"),
        P(),
        P("seq", "ch"),
        P("seq", "ch"),
        P("ch", "seq"),
    )
    out_specs = (
        P(None, "seq", None),
        P(None, "seq", "ch"),
        P(None, "seq", None),
        P(),
        P("seq", "ch"),
        P("seq", "ch"),
        P("ch", "seq"),
        P(None, "ch"),
        P("ch"),
        P("ch"),
        P("ch", None, None),
        P("ch"),
        P("ch", None, None),
        P("ch"),
        P(),
        P("seq", "ch"),
        P("seq", "ch"),
        P("ch", "seq"),
    )
    return jax.shard_map(body, mesh=mesh, in_specs=in_specs, out_specs=out_specs, check_vma=False)
```

time: 2910 us -> 782 us (0.27)
  waiting for transfers between devices: 1710 us -> 217 us
  local copies, waits for them, and re-layouts: 537 us -> 107 us
  other arithmetic: 249 us -> 53.8 us
  Pallas kernels: 0 us -> 188 us
  blocking collectives: 162 us -> 0 us
  matrix products: 210 us -> 100 us
  starting transfers between devices: 5.42 us -> 101 us
    reduce_scatter x6 -> x0, waiting for transfers between devices: 954 us -> none  [the longest x1 212 us: body(): lax.psum_scatter(grad_mlpg_w, 'seq', scatter_dimension=0, tiled=True)]
    psum x4 -> x0, waiting for transfers between devices: 451 us -> none  [the longest x1 206 us: body(): mlp_out = lax.psum(project(product, down_full), 'ch')]
    all_gather x6 -> x0, waiting for transfers between devices: 305 us -> none  [the longest x1 88.7 us: body(): lax.all_gather(low_mlp_down, 'seq', axis=1, tiled=True)]
    slice x114 -> x29, local copies, waits for them, and re-layouts: 298 us -> 14.8 us  [the longest x6 3.63 us: joined(): return (total[0:1], total[1:2].astype(LOW))]
    pallas_call x0 -> x34, Pallas kernels: none -> 188 us  [the longest x20 59.9 us: ring_step(): pl.pallas_call(kernel, grid=(grid,), in_specs=blocks + got_specs, out_spe...]
    ppermute x2 -> x78, waiting for transfers between devices: 2.42 us -> 181 us  [the longest x12 100 us: step(): self.up.append(lax.ppermute(first, 'seq', ahead))]
    pad x56 -> x0, local copies, waits for them, and re-layouts: 165 us -> none  [the longest x28 82.8 us: body(): lax.associative_scan(affine, (decay_rate, driven), axis=1)]
    all_gather x4 -> x0, blocking collectives: 123 us -> none  [prefix(): pieces = jax.tree.map(lambda part: lax.all_gather(part, axis), value)]
  transfers between devices with their start and end apart: 18 -> 83, of which waited for: 16 -> 40; matrix products, arithmetic and copies ran while one was open for 19% -> 28% of each run, Pallas kernels for 0% -> 22%
where the time goes in v1:
time: 782 us; the launch traced here: 770 us
  waiting for transfers between devices  217 us (28%)
  Pallas kernels  188 us (24%)
  local copies, waits for them, and re-layouts  107 us (14%)
  starting transfers between devices  101 us (13%)
  matrix products  100 us (13%)
  other arithmetic  53.8 us (7%)
    ppermute x12, waiting for transfers between devices, step(): self.up.append(lax.ppermute(first, 'seq', ahead))  100 us
    unnamed x227, local copies, waits for them, and re-layouts  70.9 us
    pallas_call x20, Pallas kernels, ring_step(): pl.pallas_call(kernel, grid=(grid,), in_specs=blocks + got_specs, out_spe...  59.9 us
    dot_general x6, matrix products, project(): return jnp.einsum('rtd,df->rtf', left, right, preferred_element_type=F32)  53.4 us
    ppermute x16, waiting for transfers between devices, step(): lax.ppermute(up, 'seq', ahead)  48.8 us
    dot_general x6, matrix products, outer_sum(): jnp.einsum('rtd,rtf->df', left, right, preferred_element_type=F32)  46.9 us
    pallas_call x4, Pallas kernels, back_project(): pl.pallas_call(kernel, grid=(width // tile,), in_specs=in_specs, out_spec...  46.1 us
    all_to_all x4, waiting for transfers between devices, to_all(): lax.all_to_all(jnp.broadcast_to(value[None], (count,) + value.shape), axi...  36.4 us
  transfers between devices with their start and end apart: 83, of which 40 were waited for; matrix products, arithmetic and copies ran while one was open for 28% of the time, Pallas kernels for 22%

profile of v1, /device:TPU:0, one launch (start us, length us, event | category | flops | bytes accessed | tf_op | source)
XLA Modules:
  0.0 770.0 jit_solution(15468652404417877805)
XLA Ops:
  22.5 7.9 %collective-permute-done = bf16[256,1920]{1,0:T(8,128)(2,1)} collective-permute-done((bf16[256,1920]{1,0:T(8,128)(2,1)}, bf16[256,1920]{1,0:T(8,128)(2,1)}, u32[]{:S(2)}, u32[]{:S(2)}) %collective-permute-start) | collective-permute-done | bytes 983072 | tf_op jit(solution)/shard_map/ppermute | solution.py:88
  47.8 11.4 %collective-permute-done.8.values_ref = f32[4,8,2048]{2,1,0:T(8,128)S(1)} collective-permute-done((f32[4,8,2048]{2,1,0:T(8,128)S(1)}, f32[4,8,2048]{2,1,0:T(8,128)S(1)}, u32[]{:S(2)}, u32[]{:S(2)}) %collective-permute-start.8) | collective-permute-done | bytes 262176 | tf_op jit(solution)/shard_map/ppermute | solution.py:773
  68.0 14.6 %collective-permute-done.4 = bf16[256,1920]{1,0:T(8,128)(2,1)} collective-permute-done((bf16[256,1920]{1,0:T(8,128)(2,1)}, bf16[256,1920]{1,0:T(8,128)(2,1)}, u32[]{:S(2)}, u32[]{:S(2)}) %collective-permute-start.4) | collective-permute-done | bytes 983072 | tf_op jit(solution)/shard_map/ppermute | solution.py:88
  100.6 7.3 fusion.15.input_ref.pre_ref
  107.9 14.8 %forward_scan.1 = (f32[4,256,640]{2,1,0:T(8,128)S(1)}, f32[4,256,640]{2,1,0:T(8,128)}, f32[4,256,640]{2,1,0:T(8,128)}, f32[4,256,640]{2,1,0:T(8,128)}, f32[4,256,640]{2,1,0:T(8,128)}, /*index=5*/f32[4,8,640]{2,1,0:T(8,128)S(1)}) custom-call(f32[4,256,1280]{2,1,0:T(8,128)} %fusion.15.input_ref.pre_ref, f32[4,8,1280]{2,1,0:T(8,128)S(1)} %fusion.13.halo_ref, ...), custom_call_target="tpu_custom_call" | custom-call | flops 1 | bytes 1 | tf_op jit(solution)/shard_map/forward_scan/pallas_call | solution.py:500
  143.5 5.8 fusion.22
  149.4 6.4 back_project.4
  176.4 6.7 shard_map.315
  185.7 16.6 %collective-permute-done.12 = bf16[256,3072]{1,0:T(8,128)(2,1)} collective-permute-done((bf16[256,3072]{1,0:T(8,128)(2,1)}, bf16[256,3072]{1,0:T(8,128)(2,1)}, u32[]{:S(2)}, u32[]{:S(2)}) %collective-permute-start.12) | collective-permute-done | bytes 1572896 | tf_op jit(solution)/shard_map/ppermute | solution.py:88
  213.0 25.5 %collective-permute-done.15 = bf16[256,3072]{1,0:T(8,128)(2,1)S(1)} collective-permute-done((bf16[256,3072]{1,0:T(8,128)(2,1)}, bf16[256,3072]{1,0:T(8,128)(2,1)S(1)}, u32[]{:S(2)}, u32[]{:S(2)}) %collective-permute-start.15) | collective-permute-done | bytes 1572896 | tf_op jit(solution)/shard_map/ppermute | solution.py:88
  243.5 13.5 %collective-permute-done.17 = bf16[128,3072]{1,0:T(8,128)(2,1)S(1)} collective-permute-done((bf16[128,3072]{1,0:T(8,128)(2,1)S(1)}, bf16[128,3072]{1,0:T(8,128)(2,1)S(1)}, u32[]{:S(2)}, u32[]{:S(2)}) %collective-permute-start.17) | collective-permute-done | bytes 786464 | tf_op jit(solution)/shard_map/ppermute | solution.py:88
  260.9 11.2 %fusion.11 = f32[4,256,1536]{2,1,0:T(8,128)} fusion(bf16[2048,1536]{1,0:T(8,128)(2,1)} %get-tuple-element.554.refs_2_, bf16[1,256,2048]{2,1,0:T(8,128)(2,1)S(1)} %collective-permute-done.25, bf16[1,256,2048]{2,1,0:T(8,128)(2,1)S(1)} %collective-permute-done.24, bf16[1,256,2048]{2,1,0:T(8,128)(2,1)S(1)} %collective-permute-done.23, ...), kind=kOutput, calls=%fused_computation.20 | convolution fusion | flops 6448742400 | bytes 16777216 | tf_op jit(solution)/shard_map/rtd,df->rtf/dot_general | solution.py:683
  277.1 13.0 %multiply_convert_fusion.1 = (bf16[4,256,1536]{2,1,0:T(8,128)(2,1)S(1)}, f32[4,256,1536]{2,1,0:T(8,128)}) fusion(f32[4,256,1536]{2,1,0:T(8,128)} %fusion.11, bf16[2048,1536]{1,0:T(8,128)(2,1)} %get-tuple-element.247.refs_3_, bf16[1,256,2048]{2,1,0:T(8,128)(2,1)S(1)} %collective-permute-done.25, bf16[1,256,2048]{2,1,0:T(8,128)(2,1)S(1)} %collective-permute-done.24, ...), kind=kOutput, calls=%fused_computation.23 | convolution fusion | flops 6464471040 | bytes 26214400 | tf_op jit(solution)/shard_map/rtd,df->rtf/dot_general | solution.py:683
  294.8 8.7 %bitcast_convert_fusion.2.refs_0_.refs_1_ = bf16[2048,1536]{1,0:T(8,128)(2,1)} fusion(bf16[4,256,2048]{2,1,0:T(8,128)(2,1)S(1)} %copy-done.87, bf16[4,256,1536]{2,1,0:T(8,128)(2,1)S(1)} %get-tuple-element.279.refs_0_), kind=kOutput, calls=%fused_computation.6 | convolution fusion | flops 6445596672 | bytes 13631488 | tf_op jit(solution)/shard_map/rtd,rtf->df/dot_general | solution.py:691
  314.5 7.3 collective-permute-done.28
  327.9 16.1 %multiply_convert_fusion = (bf16[4,256,1536]{2,1,0:T(8,128)(2,1)}, bf16[4,256,1536]{2,1,0:T(8,128)(2,1)S(1)}) fusion(f32[4,256,1536]{2,1,0:T(8,128)} %fusion.11, f32[4,256,1536]{2,1,0:T(8,128)} %get-tuple-element.605, bf16[4,256,2048]{2,1,0:T(8,128)(2,1)S(1)} %copy-done.88, bf16[2048,1536]{1,0:T(8,128)(2,1)} %constant_dynamic-update-slice_fusion.3.refs_1_), kind=kOutput, calls=%fused_computation.22 | convolution fusion | flops 6478626816 | bytes 29360128 | tf_op jit(solution)/shard_map/rtd,df->rtf/dot_general | solution.py:683
  348.8 18.0 %back_project.5 = (f32[2,256,2048]{2,1,0:T(8,128)}, bf16[2,256,2048]{2,1,0:T(8,128)(2,1)S(1)}) custom-call(bf16[4,256,1536]{2,1,0:T(8,128)(2,1)S(1)} %get-tuple-element.263.refs_0_, bf16[4,256,1536]{2,1,0:T(8,128)(2,1)} %get-tuple-element.535.refs_1_, bf16[2048,1536]{1,0:T(8,128)(2,1)} %get-tuple-element.554.refs_2_, ...), custom_call_target="tpu_custom_call" | custom-call | flops 1 | bytes 1 | tf_op jit(solution)/shard_map/back_project/pallas_call | solution.py:585
  374.9 11.0 %bitcast_convert_fusion.1.refs_0_.refs_1_ = bf16[2048,1536]{1,0:T(8,128)(2,1)} fusion(bf16[4,256,2048]{2,1,0:T(8,128)(2,1)} %pad_maximum_fusion, bf16[4,256,1536]{2,1,0:T(8,128)(2,1)S(1)} %get-tuple-element.263.refs_0_), kind=kOutput, calls=%fused_computation.5 | convolution fusion | flops 6445596672 | bytes 13631488 | tf_op jit(solution)/shard_map/rtd,rtf->df/dot_general | solution.py:691
  399.2 11.0 %bitcast_convert_fusion.refs_0_.refs_1_ = bf16[2048,1536]{1,0:T(8,128)(2,1)} fusion(bf16[4,256,2048]{2,1,0:T(8,128)(2,1)} %pad_maximum_fusion, bf16[4,256,1536]{2,1,0:T(8,128)(2,1)S(1)} %copy-done.67), kind=kOutput, calls=%fused_computation.4 | convolution fusion | flops 6445596672 | bytes 13631488 | tf_op jit(solution)/shard_map/rtd,rtf->df/dot_general | solution.py:691
  413.6 11.0 %back_project.6 = (f32[2,256,2048]{2,1,0:T(8,128)}, bf16[2,256,2048]{2,1,0:T(8,128)(2,1)}) custom-call(bf16[4,256,1536]{2,1,0:T(8,128)(2,1)S(1)} %copy-done.20, bf16[2048,1536]{1,0:T(8,128)(2,1)} %constant_dynamic-update-slice_fusion.3.refs_1_), custom_call_target="tpu_custom_call" | custom-call | flops 1 | bytes 1 | tf_op jit(solution)/shard_map/back_project/pallas_call | solution.py:585
  436.9 8.0 %collective-permute-done.41.refs_2_ = bf16[128,1536]{1,0:T(8,128)(2,1)S(1)} collective-permute-done((bf16[128,1536]{1,0:T(8,128)(2,1)S(1)}, bf16[128,1536]{1,0:T(8,128)(2,1)S(1)}, u32[]{:S(2)}, u32[]{:S(2)}) %collective-permute-start.41) | collective-permute-done | bytes 393248 | tf_op jit(solution)/shard_map/ppermute | solution.py:125
  474.5 12.1 %backward_scan.1 = (bf16[4,256,640]{2,1,0:T(8,128)(2,1)S(1)}, f32[4,256,640]{2,1,0:T(8,128)S(1)}, f32[4,256,640]{2,1,0:T(8,128)}, f32[4,8,640]{2,1,0:T(8,128)S(1)}) custom-call(f32[4,256,640]{2,1,0:T(8,128)} %fusion.23.mixed_ref, f32[4,256,1280]{2,1,0:T(8,128)} %fusion.15.input_ref.pre_ref, f32[4,256,640]{2,1,0:T(8,128)} %get-tuple-element.534.state_ref, ...), custom_call_target="tpu_custom_call" | custom-call | flops 1 | bytes 1 | tf_op jit(solution)/shard_map/backward_scan/pallas_call | solution.py:519
  489.2 9.1 %collective-permute-done.50.refs_2_ = bf16[256,1536]{1,0:T(8,128)(2,1)S(1)} collective-permute-done((bf16[256,1536]{1,0:T(8,128)(2,1)S(1)}, bf16[256,1536]{1,0:T(8,128)(2,1)S(1)}, u32[]{:S(2)}, u32[]{:S(2)}) %collective-permute-start.50) | collective-permute-done | bytes 786464 | tf_op jit(solution)/shard_map/ppermute | solution.py:125
  523.7 23.7 %all-to-all-done.1 = f32[8,8,640]{2,1,0:T(8,128)S(1)} async-done(((f32[8,8,640]{2,1,0:T(8,128)}), f32[8,8,640]{2,1,0:T(8,128)S(1)}, u32[]{:S(2)}, u32[]{:S(2)}) %all-to-all-start.1) | async-done | bytes 163872 | tf_op jit(solution)/shard_map/all_to_all | solution.py:243
  549.1 21.7 %branch_backward.1 = (bf16[4,256,1280]{2,1,0:T(8,128)(2,1)}, f32[4,8,640]{2,1,0:T(8,128)S(1)}, f32[4,8,640]{2,1,0:T(8,128)S(1)}, bf16[8,160,256]{2,1,0:T(8,128)(2,1)S(1)}, f32[8,640]{1,0:T(8,128)S(1)}) custom-call(f32[4,256,640]{2,1,0:T(8,128)} %copy-done.24, f32[4,256,640]{2,1,0:T(8,128)} %get-tuple-element.319.beta_ref, ...), custom_call_target="tpu_custom_call" | custom-call | flops 1 | bytes 1 | tf_op jit(solution)/shard_map/branch_backward/pallas_call | solution.py:545
  587.4 10.7 %back_project.7 = (f32[2,256,2048]{2,1,0:T(8,128)}, bf16[2,256,2048]{2,1,0:T(8,128)(2,1)}) custom-call(bf16[4,256,1280]{2,1,0:T(8,128)(2,1)S(1)} %fusion.31.refs_0_, bf16[2048,1280]{1,0:T(8,128)(2,1)} %copy-done.56), custom_call_target="tpu_custom_call" | custom-call | flops 1 | bytes 1 | tf_op jit(solution)/shard_map/back_project/pallas_call | solution.py:585
  625.8 7.8 %bitcast_convert_fusion.3.refs_2_.refs_5_ = bf16[2048,640]{1,0:T(8,128)(2,1)} fusion(bf16[4,256,2048]{2,1,0:T(8,128)(2,1)} %copy-done.16, bf16[4,256,1280]{2,1,0:T(8,128)(2,1)} %copy-done.22), kind=kOutput, calls=%fused_computation.25 | convolution fusion | flops 2685665280 | bytes 8126464 | tf_op jit(solution)/shard_map/rtd,rtf->df/dot_general | solution.py:691
  633.6 7.4 collective-permute-done.61.refs_2_
  650.3 9.8 %collective-permute-done.64.refs_6_ = bf16[128,1920]{1,0:T(8,128)(2,1)S(1)} collective-permute-done((bf16[128,1920]{1,0:T(8,128)(2,1)S(1)}, bf16[128,1920]{1,0:T(8,128)(2,1)S(1)}, u32[]{:S(2)}, u32[]{:S(2)}) %collective-permute-start.64) | collective-permute-done | bytes 491552 | tf_op jit(solution)/shard_map/ppermute | solution.py:125
  705.1 7.1 all-to-all-done.3
  717.4 8.9 %shard_map.317 = f32[4,256,2048]{2,1,0:T(8,128)} custom-call(s32[4]{0:T(128)S(1)} %copy-done.44, s32[8]{0:T(128)S(1)} %copy-done.40, f32[4,256,2048]{2,1,0:T(8,128)} %base_ref.2, bf16[1,256,2048]{2,1,0:T(8,128)(2,1)} %subtract_convert_fusion.refs_0_, bf16[1,256,2048]{2,1,0:T(8,128)(2,1)} %collective-permute-done.66.refs_1_, ...), custom_call_target="tpu_custom_call" | custom-call | flops 1 | bytes 1 | tf_op jit(solution)/shard_map/pallas_call | solution.py:641
  726.3 8.6 %shard_map.318 = f32[4,256,2048]{2,1,0:T(8,128)} custom-call(s32[4]{0:T(128)S(1)} %copy-done.44, s32[8]{0:T(128)S(1)} %copy-done.40, f32[4,256,2048]{2,1,0:T(8,128)} %base_ref.3, bf16[1,256,2048]{2,1,0:T(8,128)(2,1)S(1)} %copy-done.18, bf16[1,256,2048]{2,1,0:T(8,128)(2,1)} %collective-permute-done.71.refs_1_, ...), custom_call_target="tpu_custom_call" | custom-call | flops 1 | bytes 1 | tf_op jit(solution)/shard_map/pallas_call | solution.py:641
  (538 shorter events, 395.0 us)
Async XLA Ops:
  31.9 28.4 %collective-permute-start.2 = (bf16[256,1920]{1,0:T(8,128)(2,1)}, bf16[256,1920]{1,0:T(8,128)(2,1)}, u32[]{:S(2)}, u32[]{:S(2)}) collective-permute-start(bf16[256,1920]{1,0:T(8,128)(2,1)} %collective-permute-done), channel_id=1, source_target_pairs={{0,8},{8,16},{16,24},{24,28},{28,20},{20,12},{12,4},{4,0},{1,9},{9... | collective-permute-start | bytes 2949128 | tf_op jit(solution)/shard_map/ppermute | solution.py:88
  97.6 31.4 %collective-permute-start.9 = (bf16[256,3072]{1,0:T(8,128)(2,1)}, bf16[256,3072]{1,0:T(8,128)(2,1)}, u32[]{:S(2)}, u32[]{:S(2)}) collective-permute-start(bf16[256,3072]{1,0:T(8,128)(2,1)} %pad_maximum_fusion.1), channel_id=1, source_target_pairs={{0,8},{8,16},{16,24},{24,28},{28,20},{20,12},{12,4},{4,0},{1,9},{9... | collective-permute-start | bytes 4718600 | tf_op jit(solution)/shard_map/ppermute | solution.py:88
  98.3 32.1 %collective-permute-start.10 = (bf16[256,3072]{1,0:T(8,128)(2,1)}, bf16[256,3072]{1,0:T(8,128)(2,1)}, u32[]{:S(2)}, u32[]{:S(2)}) collective-permute-start(bf16[256,3072]{1,0:T(8,128)(2,1)} %pad_maximum_fusion.1), channel_id=1, source_target_pairs={{8,0},{16,8},{24,16},{28,24},{20,28},{12,20},{4,12},{0,4},{9,1},{1... | collective-permute-start | bytes 4718600 | tf_op jit(solution)/shard_map/ppermute | solution.py:89
  165.1 37.1 %collective-permute-start.12 = (bf16[256,3072]{1,0:T(8,128)(2,1)}, bf16[256,3072]{1,0:T(8,128)(2,1)}, u32[]{:S(2)}, u32[]{:S(2)}) collective-permute-start(bf16[256,3072]{1,0:T(8,128)(2,1)} %collective-permute-done.9), channel_id=1, source_target_pairs={{0,8},{8,16},{16,24},{24,28},{28,20},{20,12},{12,4},{4,0},{1,9},{9... | collective-permute-start | bytes 4718600 | tf_op jit(solution)/shard_map/ppermute | solution.py:88
  165.1 37.1 %collective-permute-start.13 = (bf16[256,3072]{1,0:T(8,128)(2,1)}, bf16[256,3072]{1,0:T(8,128)(2,1)}, u32[]{:S(2)}, u32[]{:S(2)}) collective-permute-start(bf16[256,3072]{1,0:T(8,128)(2,1)} %collective-permute-done.10), channel_id=1, source_target_pairs={{8,0},{16,8},{24,16},{28,24},{20,28},{12,20},{4,12},{0,4},{9,1},{1... | collective-permute-start | bytes 4718600 | tf_op jit(solution)/shard_map/ppermute | solution.py:89
  172.2 34.7 %collective-permute-start.14 = (bf16[1,256,2048]{2,1,0:T(8,128)(2,1)S(1)}, bf16[1,256,2048]{2,1,0:T(8,128)(2,1)}, u32[]{:S(2)}, u32[]{:S(2)}) collective-permute-start(bf16[1,256,2048]{2,1,0:T(8,128)(2,1)S(1)} %slice.743), channel_id=1, source_target_pairs={{0,2},{1,3},{2,0},{3,1},{4,6},{5,7},{6,4},{7,5},{8,10},{9,11},{10,... | collective-permute-start | bytes 3145736 | tf_op jit(solution)/shard_map/ppermute | solution.py:209
  202.2 36.2 %collective-permute-start.15 = (bf16[256,3072]{1,0:T(8,128)(2,1)}, bf16[256,3072]{1,0:T(8,128)(2,1)S(1)}, u32[]{:S(2)}, u32[]{:S(2)}) collective-permute-start(bf16[256,3072]{1,0:T(8,128)(2,1)} %collective-permute-done.12), channel_id=1, source_target_pairs={{0,8},{8,16},{16,24},{24,28},{28,20},{20,12},{12,4},{4,0},{1,9},{9... | collective-permute-start | bytes 4718600 | tf_op jit(solution)/shard_map/ppermute | solution.py:88
  202.8 35.8 %collective-permute-start.16 = (bf16[256,3072]{1,0:T(8,128)(2,1)}, bf16[256,3072]{1,0:T(8,128)(2,1)S(1)}, u32[]{:S(2)}, u32[]{:S(2)}) collective-permute-start(bf16[256,3072]{1,0:T(8,128)(2,1)} %collective-permute-done.13), channel_id=1, source_target_pairs={{8,0},{16,8},{24,16},{28,24},{20,28},{12,20},{4,12},{0,4},{9,1},{1... | collective-permute-start | bytes 4718600 | tf_op jit(solution)/shard_map/ppermute | solution.py:89
  208.8 33.3 %collective-permute-start.23 = (bf16[1,256,2048]{2,1,0:T(8,128)(2,1)S(1)}, bf16[1,256,2048]{2,1,0:T(8,128)(2,1)S(1)}, u32[]{:S(2)}, u32[]{:S(2)}) collective-permute-start(bf16[1,256,2048]{2,1,0:T(8,128)(2,1)S(1)} %multiply_convert_fusion.2), channel_id=1, source_target_pairs={{0,2},{1,3},{2,0},{3,1},{4,6},{5,7},{6,4},{7,5},{8,10},{9,11},{10,... | collective-permute-start | bytes 3145736 | tf_op jit(solution)/shard_map/ppermute | solution.py:209
  213.0 47.9 %collective-permute-start.24 = (bf16[1,256,2048]{2,1,0:T(8,128)(2,1)S(1)}, bf16[1,256,2048]{2,1,0:T(8,128)(2,1)S(1)}, u32[]{:S(2)}, u32[]{:S(2)}) collective-permute-start(bf16[1,256,2048]{2,1,0:T(8,128)(2,1)S(1)} %multiply_convert_fusion.2), channel_id=1, source_target_pairs={{0,1},{1,0},{2,3},{3,2},{4,5},{5,4},{6,7},{7,6},{8,9},{9,8},{10,11... | collective-permute-start | bytes 3145736 | tf_op jit(solution)/shard_map/ppermute | solution.py:205
  392.9 31.8 %collective-permute-start.37 = (bf16[1,256,2048]{2,1,0:T(8,128)(2,1)}, bf16[1,256,2048]{2,1,0:T(8,128)(2,1)}, u32[]{:S(2)}, u32[]{:S(2)}) collective-permute-start(bf16[1,256,2048]{2,1,0:T(8,128)(2,1)} %slice.742), channel_id=1, source_target_pairs={{0,2},{1,3},{2,0},{3,1},{4,6},{5,7},{6,4},{7,5},{8,10},{9,11},{10,... | collective-permute-start | bytes 3145736 | tf_op jit(solution)/shard_map/ppermute | solution.py:209
  396.9 27.8 %collective-permute-start.38 = (bf16[256,1536]{1,0:T(8,128)(2,1)S(1)}, bf16[256,1536]{1,0:T(8,128)(2,1)S(1)}, u32[]{:S(2)}, u32[]{:S(2)}) collective-permute-start(bf16[256,1536]{1,0:T(8,128)(2,1)S(1)} %get-tuple-element.276), channel_id=1, source_target_pairs={{0,8},{8,16},{16,24},{24,28},{28,20},{20,12},{12,4},{4,0},{1,9},{9... | collective-permute-start | bytes 2359304 | tf_op jit(solution)/shard_map/ppermute | solution.py:125
  446.3 64.1 %collective-permute-start.47 = (bf16[2,256,2048]{2,1,0:T(8,128)(2,1)}, bf16[2,256,2048]{2,1,0:T(8,128)(2,1)}, u32[]{:S(2)}, u32[]{:S(2)}) collective-permute-start(bf16[2,256,2048]{2,1,0:T(8,128)(2,1)} %get-tuple-element.304), channel_id=1, source_target_pairs={{0,1},{1,0},{2,3},{3,2},{4,5},{5,4},{6,7},{7,6},{8,9},{9,8},{10,11... | collective-permute-start | bytes 6291464 | tf_op jit(solution)/shard_map/ppermute | solution.py:205
  461.2 28.0 %collective-permute-start.48 = (bf16[256,1536]{1,0:T(8,128)(2,1)}, bf16[256,1536]{1,0:T(8,128)(2,1)S(1)}, u32[]{:S(2)}, u32[]{:S(2)}) collective-permute-start(bf16[256,1536]{1,0:T(8,128)(2,1)} %copy-done.50), channel_id=1, source_target_pairs={{0,8},{8,16},{16,24},{24,28},{28,20},{20,12},{12,4},{4,0},{1,9},{9... | collective-permute-start | bytes 2359304 | tf_op jit(solution)/shard_map/ppermute | solution.py:125
  464.5 33.7 %collective-permute-start.50 = (bf16[256,1536]{1,0:T(8,128)(2,1)S(1)}, bf16[256,1536]{1,0:T(8,128)(2,1)S(1)}, u32[]{:S(2)}, u32[]{:S(2)}) collective-permute-start(bf16[256,1536]{1,0:T(8,128)(2,1)S(1)} %copy-done.49), channel_id=1, source_target_pairs={{0,8},{8,16},{16,24},{24,28},{28,20},{20,12},{12,4},{4,0},{1,9},{9... | collective-permute-start | bytes 2359304 | tf_op jit(solution)/shard_map/ppermute | solution.py:125
  466.7 32.0 %collective-permute-start.51 = (bf16[256,1536]{1,0:T(8,128)(2,1)S(1)}, bf16[256,1536]{1,0:T(8,128)(2,1)S(1)}, u32[]{:S(2)}, u32[]{:S(2)}) collective-permute-start(bf16[256,1536]{1,0:T(8,128)(2,1)S(1)} %copy-done.46), channel_id=1, source_target_pairs={{8,0},{16,8},{24,16},{28,24},{20,28},{12,20},{4,12},{0,4},{9,1},{1... | collective-permute-start | bytes 2359304 | tf_op jit(solution)/shard_map/ppermute | solution.py:125
  506.2 65.5 %collective-permute-start.53 = (bf16[256,1536]{1,0:T(8,128)(2,1)}, bf16[256,1536]{1,0:T(8,128)(2,1)}, u32[]{:S(2)}, u32[]{:S(2)}) collective-permute-start(bf16[256,1536]{1,0:T(8,128)(2,1)} %get-tuple-element.311), channel_id=1, source_target_pairs={{0,8},{8,16},{16,24},{24,28},{28,20},{20,12},{12,4},{4,0},{1,9},{9... | collective-permute-start | bytes 2359304 | tf_op jit(solution)/shard_map/ppermute | solution.py:125
  507.5 64.3 %collective-permute-start.54 = (bf16[256,1536]{1,0:T(8,128)(2,1)}, bf16[256,1536]{1,0:T(8,128)(2,1)}, u32[]{:S(2)}, u32[]{:S(2)}) collective-permute-start(bf16[256,1536]{1,0:T(8,128)(2,1)} %get-tuple-element.312), channel_id=1, source_target_pairs={{8,0},{16,8},{24,16},{28,24},{20,28},{12,20},{4,12},{0,4},{9,1},{1... | collective-permute-start | bytes 2359304 | tf_op jit(solution)/shard_map/ppermute | solution.py:125
  508.3 63.5 %collective-permute-start.55 = (bf16[256,1536]{1,0:T(8,128)(2,1)}, bf16[256,1536]{1,0:T(8,128)(2,1)}, u32[]{:S(2)}, u32[]{:S(2)}) collective-permute-start(bf16[256,1536]{1,0:T(8,128)(2,1)} %get-tuple-element.315), channel_id=1, source_target_pairs={{0,8},{8,16},{16,24},{24,28},{28,20},{20,12},{12,4},{4,0},{1,9},{9... | collective-permute-start | bytes 2359304 | tf_op jit(solution)/shard_map/ppermute | solution.py:125
  509.5 62.3 %collective-permute-start.56 = (bf16[256,1536]{1,0:T(8,128)(2,1)}, bf16[256,1536]{1,0:T(8,128)(2,1)}, u32[]{:S(2)}, u32[]{:S(2)}) collective-permute-start(bf16[256,1536]{1,0:T(8,128)(2,1)} %get-tuple-element.316), channel_id=1, source_target_pairs={{8,0},{16,8},{24,16},{28,24},{20,28},{12,20},{4,12},{0,4},{9,1},{1... | collective-permute-start | bytes 2359304 | tf_op jit(solution)/shard_map/ppermute | solution.py:125
  511.0 36.3 %all-to-all-start.1 = ((f32[8,8,640]{2,1,0:T(8,128)}), f32[8,8,640]{2,1,0:T(8,128)S(1)}, u32[]{:S(2)}, u32[]{:S(2)}) async-start(f32[8,8,640]{2,1,0:T(8,128)} %broadcast_in_dim.83), calls=%async_computation.1 | async-start | bytes 327680 | tf_op jit(solution)/shard_map/all_to_all | solution.py:243
  522.1 49.6 %collective-permute-start.52 = (bf16[1,256,2048]{2,1,0:T(8,128)(2,1)}, bf16[1,256,2048]{2,1,0:T(8,128)(2,1)}, u32[]{:S(2)}, u32[]{:S(2)}) collective-permute-start(bf16[1,256,2048]{2,1,0:T(8,128)(2,1)} %slice.741), channel_id=1, source_target_pairs={{0,2},{1,3},{2,0},{3,1},{4,6},{5,7},{6,4},{7,5},{8,10},{9,11},{10,... | collective-permute-start | bytes 3145736 | tf_op jit(solution)/shard_map/ppermute | solution.py:209
  614.5 31.9 %collective-permute-start.63 = (bf16[1,256,2048]{2,1,0:T(8,128)(2,1)}, bf16[1,256,2048]{2,1,0:T(8,128)(2,1)}, u32[]{:S(2)}, u32[]{:S(2)}) collective-permute-start(bf16[1,256,2048]{2,1,0:T(8,128)(2,1)} %slice.740), channel_id=1, source_target_pairs={{0,2},{1,3},{2,0},{3,1},{4,6},{5,7},{6,4},{7,5},{8,10},{9,11},{10,... | collective-permute-start | bytes 3145736 | tf_op jit(solution)/shard_map/ppermute | solution.py:209
  619.1 69.9 %collective-permute-start.71 = (bf16[1,256,2048]{2,1,0:T(8,128)(2,1)}, bf16[1,256,2048]{2,1,0:T(8,128)(2,1)}, u32[]{:S(2)}, u32[]{:S(2)}) collective-permute-start(bf16[1,256,2048]{2,1,0:T(8,128)(2,1)} %get-tuple-element.538.refs_0_), channel_id=1, source_target_pairs={{0,2},{1,3},{2,0},{3,1},{4,6},{5,7},{6,4},{7,5},{8,10},{9,11},{10,... | collective-permute-start | bytes 3145736 | tf_op jit(solution)/shard_map/ppermute | solution.py:209
  621.6 51.4 %all-to-all-start.2 = ((bf16[8,163,256]{2,1,0:T(8,128)(2,1)}), bf16[8,163,256]{2,1,0:T(8,128)(2,1)}, u32[]{:S(2)}, u32[]{:S(2)}) async-start(bf16[8,163,256]{2,1,0:T(8,128)(2,1)} %reshape.200), calls=%async_computation.2 | async-start | bytes 1376256 | tf_op jit(solution)/shard_map/all_to_all | solution.py:891
  673.0 30.8 %collective-permute-start.69 = (bf16[1,256,2048]{2,1,0:T(8,128)(2,1)}, bf16[1,256,2048]{2,1,0:T(8,128)(2,1)S(1)}, u32[]{:S(2)}, u32[]{:S(2)}) collective-permute-start(bf16[1,256,2048]{2,1,0:T(8,128)(2,1)} %subtract_convert_fusion.refs_0_), channel_id=1, source_target_pairs={{0,1},{1,0},{2,3},{3,2},{4,5},{5,4},{6,7},{7,6},{8,9},{9,8},{10,11... | collective-permute-start | bytes 3145736 | tf_op jit(solution)/shard_map/ppermute | solution.py:205
  675.1 37.1 %all-to-all-start.3 = ((bf16[8,163,256]{2,1,0:T(8,128)(2,1)}), bf16[8,163,256]{2,1,0:T(8,128)(2,1)}, u32[]{:S(2)}, u32[]{:S(2)}) async-start(bf16[8,163,256]{2,1,0:T(8,128)(2,1)} %broadcast_in_dim.85), calls=%async_computation.3 | async-start | bytes 1376256 | tf_op jit(solution)/shard_map/all_to_all | solution.py:243
  689.0 37.3 %collective-permute-start.72 = (bf16[1,256,2048]{2,1,0:T(8,128)(2,1)S(1)}, bf16[1,256,2048]{2,1,0:T(8,128)(2,1)S(1)}, u32[]{:S(2)}, u32[]{:S(2)}) collective-permute-start(bf16[1,256,2048]{2,1,0:T(8,128)(2,1)S(1)} %copy-done.18), channel_id=1, source_target_pairs={{0,1},{1,0},{2,3},{3,2},{4,5},{5,4},{6,7},{7,6},{8,9},{9,8},{10,11... | collective-permute-start | bytes 3145736 | tf_op jit(solution)/shard_map/ppermute | solution.py:205
  690.1 36.2 %collective-permute-start.73 = (bf16[1,256,2048]{2,1,0:T(8,128)(2,1)}, bf16[1,256,2048]{2,1,0:T(8,128)(2,1)}, u32[]{:S(2)}, u32[]{:S(2)}) collective-permute-start(bf16[1,256,2048]{2,1,0:T(8,128)(2,1)} %collective-permute-done.71.refs_1_), channel_id=1, source_target_pairs={{0,1},{1,0},{2,3},{3,2},{4,5},{5,4},{6,7},{7,6},{8,9},{9,8},{10,11... | collective-permute-start | bytes 3145736 | tf_op jit(solution)/shard_map/ppermute | solution.py:205
  703.1 31.8 %collective-permute-start.74 = (bf16[256,1920]{1,0:T(8,128)(2,1)}, bf16[256,1920]{1,0:T(8,128)(2,1)}, u32[]{:S(2)}, u32[]{:S(2)}) collective-permute-start(bf16[256,1920]{1,0:T(8,128)(2,1)} %get-tuple-element.366), channel_id=1, source_target_pairs={{0,8},{8,16},{16,24},{24,28},{28,20},{20,12},{12,4},{4,0},{1,9},{9... | collective-permute-start | bytes 2949128 | tf_op jit(solution)/shard_map/ppermute | solution.py:125
  703.8 31.1 %collective-permute-start.75 = (bf16[256,1920]{1,0:T(8,128)(2,1)}, bf16[256,1920]{1,0:T(8,128)(2,1)}, u32[]{:S(2)}, u32[]{:S(2)}) collective-permute-start(bf16[256,1920]{1,0:T(8,128)(2,1)} %get-tuple-element.367), channel_id=1, source_target_pairs={{8,0},{16,8},{24,16},{28,24},{20,28},{12,20},{4,12},{0,4},{9,1},{1... | collective-permute-start | bytes 2949128 | tf_op jit(solution)/shard_map/ppermute | solution.py:125
  713.1 33.0 %all-to-all-start.4 = ((f32[32,16,256]{2,1,0:T(8,128)}), f32[32,16,256]{2,1,0:T(8,128)}, u32[]{:S(2)}, u32[]{:S(2)}) async-start(f32[32,16,256]{2,1,0:T(8,128)} %broadcast_in_dim.86), calls=%async_computation.4 | async-start | bytes 1048576 | tf_op jit(solution)/shard_map/all_to_all | solution.py:243
  (143 other events, 2707.7 us)

commit v2 on v1

--- a/solution.py
+++ b/solution.py
@@ -139,7 +139,7 @@
     half, rows = count // 2, fulls[0].shape[0] // count
     widths = [full.shape[1] for full in fulls]
     total = sum(widths)
-    parts = 4
+    parts = 2
     piece = rows // parts
     first, last = step == half, step == 0
 
@@ -829,27 +829,29 @@
     kept, away = back_project([after_that(grad_mlp, sent), grad_up], [mlp_gate_full, mlp_up_full])
     away = meet(away, reduce_down)
     sent = reduce_down.step()
-    came = to_near(away)
-    mlp_gate_part = outer_sum(after_that(hidden_two, (sent, away)), grad_mlp)
-    kept, beyond = joined(kept, after_that(came, mlp_gate_part))
-    beyond = meet(beyond, reduce_down)
+    kept, beyond = joined(kept, after_that(to_near(away), sent))
+    arrived = to_far(beyond)
+    mlp_gate_part = outer_sum(after_that(hidden_two, beyond), grad_mlp)
+    mlp_gate_part = meet(mlp_gate_part, reduce_down)
     sent = reduce_down.step()
-    arrived = to_far(beyond)
-    mlp_up_part = outer_sum(after_that(hidden_two, (sent, beyond)), grad_up)
-    result_kept, result_away = back_project([after_that(product, mlp_up_part)], [mlp_down_full])
-    arrived = meet(after_that(arrived, result_away), reduce_down)
-    reduce_gate = Reduce([mlp_gate_part], reduce_down.latest)
-    reduce_up = Reduce([mlp_up_part], reduce_down.latest)
-    sent = (reduce_gate.step(), reduce_up.step())
+    arrived = after_that(arrived, sent)
     back_two, share_two = norm_back(kept + arrived.astype(F32), after, root_two, gain_two)
     grad_after = cotangent_own + back_two
-    own = after_that(grad_after.astype(LOW), sent)
+    own = grad_after.astype(LOW)
     far, near = to_far(own), to_near(own)
-    result_came = to_near(after_that(result_away, own))
+    mlp_up_part = outer_sum(after_that(hidden_two, own), grad_up)
+    mlp_up_part = meet(mlp_up_part, reduce_down)
+    reduce_gate = Reduce([mlp_gate_part], reduce_down.latest)
+    sent = reduce_gate.step()
+    result_kept, result_away = back_project(
+        [after_that(product, (sent, mlp_up_part))], [mlp_down_full]
+    )
     (grad_down,) = reduce_down.sums()
-    grad_down = meet(grad_down, reduce_gate, reduce_up)
-    sent = (reduce_gate.step(), reduce_up.step())
+    result_away = meet(result_away, reduce_gate)
+    reduce_up = Reduce([mlp_up_part], reduce_gate.latest)
+    sent = (reduce_up.step(), reduce_gate.step())
     far = after_that(far, sent)
+    result_came = to_near(after_that(result_away, far))
     grad_one = jnp.concatenate([own, far, near, to_near(far)], axis=0)
 
     grad_mixed = project(after_that(grad_one, sent), output_full)
@@ -857,16 +859,18 @@
         grad_mixed, pre, state, recur, masks, coef
     )
     export = meet(export, reduce_gate, reduce_up)
-    sent = (reduce_gate.step(), reduce_up.step())
-    result_kept, result_beyond = joined(result_kept, after_that(result_came, (export, sent)))
-    result_arrived = to_far(result_beyond)
-    incoming = after_that(carried(export, True), result_beyond)[:, None, :]
+    incoming = carried(export, True)[:, None, :]
+    result_kept, result_beyond = joined(result_kept, after_that(result_came, export))
+    incoming = after_that(incoming, result_beyond)
+    reduce_gate.others = reduce_up.others = incoming
+    sent = (reduce_up.step(), reduce_gate.step())
+    result_arrived = to_far(after_that(result_beyond, incoming))
     grad_pre, tail, head, gate_grads, sums = run_backward(
         tail_decay, grad_part, incoming, state, carry, recur, gate, conv, pre, halo, masks,
         conv_weight, coef, high, low, grad_pre_gate,
     )
-    head = meet(after_that(head, result_arrived), reduce_gate, reduce_up)
-    sent = reduce_gate.step()
+    head = meet(after_that(head, result_arrived), reduce_up)
+    sent = reduce_up.step()
     beyond = lax.ppermute(head, "seq", [(s + 1, s) for s in range(seq_count - 1)])
     result_delta = after + (result_kept + after_that(result_arrived, (sent, head)).astype(F32))
     result_delta = (result_delta - tokens_own).astype(LOW)
@@ -875,11 +879,18 @@
     beyond = after_that(beyond, out_part)
     grad_pre = lax.dynamic_update_slice(grad_pre, (tail + beyond).astype(LOW), (0, length - 8, 0))
     kept, away = back_project([grad_pre], [in_gate])
-    away = meet(away, reduce_gate)
-    reduce_up.others = away
-    sent = reduce_up.step()
+    away = meet(away, reduce_gate, reduce_up)
+    reduce_gate.others = away
+    sent = reduce_gate.step()
     came = to_near(away)
     gate_part = outer_sum(after_that(hidden_one, sent), grad_pre_gate)
+    kept, beyond = joined(kept, after_that(came, gate_part))
+    beyond = meet(beyond, reduce_gate)
+    arrived = to_far(beyond)
+    reduce_up.others = beyond
+    sent = reduce_up.step()
+
+    in_part = outer_sum(after_that(hidden_one, (sent, beyond)), grad_pre[:, :, :channels])
     sum_rows = sums.astype(LOW).reshape(-1, WINDOW)
     small = jnp.concatenate(
         [
@@ -887,16 +898,12 @@
             jnp.pad(sum_rows, ((0, -sum_rows.shape[0] % seq_count), (0, 0))),
         ]
     )
-    small = after_that(small.reshape(seq_count, -1, WINDOW), away)
+    small = after_that(small.reshape(seq_count, -1, WINDOW), in_part)
+    in_part = after_that(in_part, small)
     small = lax.all_to_all(small, "seq", 0, 0, tiled=True)
-    small = jnp.sum(small.astype(F32), axis=0)
-    kept, beyond = joined(kept, after_that(came, gate_part))
-    arrived = to_far(beyond)
-    every = to_all(after_that(small, beyond).astype(LOW), "seq")
-    result_pieces = [result_delta, result_far, result_near, to_near(after_that(result_far, beyond))]
-
-    in_part = outer_sum(after_that(hidden_one, beyond), grad_pre[:, :, :channels])
-    in_part = meet(in_part, reduce_up)
+    small = jnp.sum(small.astype(F32), axis=0).astype(LOW)
+    every = to_all(small, "seq")
+    in_part = meet(in_part, reduce_gate, reduce_up)
     reduce_branch = Reduce([out_part, gate_part, in_part], reduce_up.latest)
     sent = reduce_branch.step()
 
@@ -916,6 +923,9 @@
     sent = reduce_branch.step()
     late_maps = after_that(maps, (sent, far))
     token_grad = assemble(cotangent, [own, far, near, to_near(far)], late_maps)
+    result_pieces = [
+        result_delta, result_far, result_near, to_near(after_that(result_far, beyond)),
+    ]
     late_maps = after_that(maps, token_grad)
     result = assemble(tokens, result_pieces, late_maps)
     result = meet(result, reduce_branch)

time: 782 us -> 737 us (0.942)
  Pallas kernels: 188 us -> 169 us
  waiting for transfers between devices: 217 us -> 201 us
  matrix products: 100 us -> 91.3 us
    all_to_all x4, waiting for transfers between devices: 36.4 us -> 16.2 us  [to_all(): lax.all_to_all(jnp.broadcast_to(value[None], (count,) + value.shape), axi...]
    pallas_call x20, Pallas kernels: 59.9 us -> 41.2 us  [ring_step(): pl.pallas_call(kernel, grid=(grid,), in_specs=blocks + got_specs, out_spe...]
    ppermute x8, waiting for transfers between devices: 0.02 us -> 10.6 us  [to_far(): return lax.ppermute(value, 'ch', far_pairs(lax.axis_size('ch')))]
    ppermute x16, waiting for transfers between devices: 48.8 us -> 40.5 us  [step(): lax.ppermute(up, 'seq', ahead)]
    unnamed x227 -> x270, local copies, waits for them, and re-layouts: 70.9 us -> 72.9 us
  transfers between devices with their start and end apart: 83 -> 83, of which waited for: 40 -> 38; matrix products, arithmetic and copies ran while one was open for 28% -> 29% of each run, Pallas kernels for 22% -> 22%
where the time goes in v2:
time: 737 us; the launch traced here: 726 us
  waiting for transfers between devices  201 us (27%)
  Pallas kernels  169 us (23%)
  local copies, waits for them, and re-layouts  106 us (14%)
  starting transfers between devices  99.2 us (13%)
  matrix products  91.3 us (12%)
  other arithmetic  55.7 us (8%)
    ppermute x12, waiting for transfers between devices, step(): self.up.append(lax.ppermute(first, 'seq', ahead))  103 us
    unnamed x270, local copies, waits for them, and re-layouts  72.9 us
    dot_general x6, matrix products, project(): return jnp.einsum('rtd,df->rtf', left, right, preferred_element_type=F32)  48.3 us
    pallas_call x4, Pallas kernels, back_project(): pl.pallas_call(kernel, grid=(width // tile,), in_specs=in_specs, out_spec...  46 us
    dot_general x6, matrix products, outer_sum(): jnp.einsum('rtd,rtf->df', left, right, preferred_element_type=F32)  43 us
    pallas_call x20, Pallas kernels, ring_step(): pl.pallas_call(kernel, grid=(grid,), in_specs=blocks + got_specs, out_spe...  41.2 us
    ppermute x16, waiting for transfers between devices, step(): lax.ppermute(up, 'seq', ahead)  40.5 us
    pallas_call x6, Pallas kernels, arranged(): pl.pallas_call(kernel, grid_spec=pltpu.PrefetchScalarGridSpec(num_scalar_...  33 us
  transfers between devices with their start and end apart: 83, of which 38 were waited for; matrix products, arithmetic and copies ran while one was open for 29% of the time, Pallas kernels for 22%

profile of v2, /device:TPU:0, one launch (start us, length us, event | category | flops | bytes accessed | tf_op | source)
XLA Modules:
  0.0 726.1 jit_solution(4120775391335330181)
XLA Ops:
  22.5 7.9 %collective-permute-done = bf16[256,1920]{1,0:T(8,128)(2,1)} collective-permute-done((bf16[256,1920]{1,0:T(8,128)(2,1)}, bf16[256,1920]{1,0:T(8,128)(2,1)}, u32[]{:S(2)}, u32[]{:S(2)}) %collective-permute-start) | collective-permute-done | bytes 983072 | tf_op jit(solution)/shard_map/ppermute | solution.py:88
  47.8 11.4 %collective-permute-done.8.values_ref = f32[4,8,2048]{2,1,0:T(8,128)S(1)} collective-permute-done((f32[4,8,2048]{2,1,0:T(8,128)S(1)}, f32[4,8,2048]{2,1,0:T(8,128)S(1)}, u32[]{:S(2)}, u32[]{:S(2)}) %collective-permute-start.8) | collective-permute-done | bytes 262176 | tf_op jit(solution)/shard_map/ppermute | solution.py:773
  68.0 14.6 %collective-permute-done.4 = bf16[256,1920]{1,0:T(8,128)(2,1)} collective-permute-done((bf16[256,1920]{1,0:T(8,128)(2,1)}, bf16[256,1920]{1,0:T(8,128)(2,1)}, u32[]{:S(2)}, u32[]{:S(2)}) %collective-permute-start.4) | collective-permute-done | bytes 983072 | tf_op jit(solution)/shard_map/ppermute | solution.py:88
  100.6 7.3 %fusion.15.input_ref.pre_ref = f32[4,256,1280]{2,1,0:T(8,128)} fusion(bf16[4,256,2048]{2,1,0:T(8,128)(2,1)S(1)} %shard_map.313, bf16[2048,1280]{1,0:T(8,128)(2,1)S(1)} %slice_dynamic-update-slice_fusion.28.refs_1_), kind=kOutput, calls=%fused_computation.30 | convolution fusion | flops 5368709120 | bytes 14680064 | tf_op jit(solution)/shard_map/rtd,df->rtf/dot_general | solution.py:683
  108.0 14.9 %forward_scan.1 = (f32[4,256,640]{2,1,0:T(8,128)S(1)}, f32[4,256,640]{2,1,0:T(8,128)}, f32[4,256,640]{2,1,0:T(8,128)}, f32[4,256,640]{2,1,0:T(8,128)}, f32[4,256,640]{2,1,0:T(8,128)}, /*index=5*/f32[4,8,640]{2,1,0:T(8,128)S(1)}) custom-call(f32[4,256,1280]{2,1,0:T(8,128)} %fusion.15.input_ref.pre_ref, f32[4,8,1280]{2,1,0:T(8,128)S(1)} %fusion.13.halo_ref, ...), custom_call_target="tpu_custom_call" | custom-call | flops 1 | bytes 1 | tf_op jit(solution)/shard_map/forward_scan/pallas_call | solution.py:500
  137.0 5.6 all-to-all-done
  143.5 5.9 fusion.22
  149.4 6.4 back_project.4
  178.8 6.9 shard_map.315
  185.7 16.5 %collective-permute-done.12 = bf16[256,3072]{1,0:T(8,128)(2,1)} collective-permute-done((bf16[256,3072]{1,0:T(8,128)(2,1)}, bf16[256,3072]{1,0:T(8,128)(2,1)}, u32[]{:S(2)}, u32[]{:S(2)}) %collective-permute-start.12) | collective-permute-done | bytes 1572896 | tf_op jit(solution)/shard_map/ppermute | solution.py:88
  212.8 25.7 %collective-permute-done.15 = bf16[256,3072]{1,0:T(8,128)(2,1)S(1)} collective-permute-done((bf16[256,3072]{1,0:T(8,128)(2,1)}, bf16[256,3072]{1,0:T(8,128)(2,1)S(1)}, u32[]{:S(2)}, u32[]{:S(2)}) %collective-permute-start.15) | collective-permute-done | bytes 1572896 | tf_op jit(solution)/shard_map/ppermute | solution.py:88
  242.9 14.0 %collective-permute-done.17 = bf16[128,3072]{1,0:T(8,128)(2,1)S(1)} collective-permute-done((bf16[128,3072]{1,0:T(8,128)(2,1)S(1)}, bf16[128,3072]{1,0:T(8,128)(2,1)S(1)}, u32[]{:S(2)}, u32[]{:S(2)}) %collective-permute-start.17) | collective-permute-done | bytes 786464 | tf_op jit(solution)/shard_map/ppermute | solution.py:88
  260.7 8.6 %fusion.11 = f32[4,256,1536]{2,1,0:T(8,128)} fusion(bf16[2048,1536]{1,0:T(8,128)(2,1)S(1)} %get-tuple-element.571.refs_2_, bf16[1,256,2048]{2,1,0:T(8,128)(2,1)S(1)} %collective-permute-done.25, bf16[1,256,2048]{2,1,0:T(8,128)(2,1)S(1)} %collective-permute-done.24, bf16[1,256,2048]{2,1,0:T(8,128)(2,1)S(1)} %collective-permute-done.23, ...), kind=kOutput, calls=%fused_computation.20 | convolution fusion | flops 6448742400 | bytes 16777216 | tf_op jit(solution)/shard_map/rtd,df->rtf/dot_general | solution.py:683
  269.3 5.4 collective-permute-done.19
  276.8 10.5 %multiply_convert_fusion.1 = (bf16[4,256,1536]{2,1,0:T(8,128)(2,1)S(1)}, f32[4,256,1536]{2,1,0:T(8,128)}) fusion(f32[4,256,1536]{2,1,0:T(8,128)} %fusion.11, bf16[2048,1536]{1,0:T(8,128)(2,1)S(1)} %copy-done.82, bf16[1,256,2048]{2,1,0:T(8,128)(2,1)S(1)} %collective-permute-done.25, bf16[1,256,2048]{2,1,0:T(8,128)(2,1)S(1)} %collective-permute-done.24, ...), kind=kOutput, calls=%fused_computation.23 | convolution fusion | flops 6464471040 | bytes 26214400 | tf_op jit(solution)/shard_map/rtd,df->rtf/dot_general | solution.py:683
  294.8 11.0 %bitcast_convert_fusion.2.refs_0_.refs_1_ = bf16[2048,1536]{1,0:T(8,128)(2,1)} fusion(bf16[4,256,2048]{2,1,0:T(8,128)(2,1)} %get-tuple-element.257, bf16[4,256,1536]{2,1,0:T(8,128)(2,1)S(1)} %get-tuple-element.298.refs_0_), kind=kOutput, calls=%fused_computation.6 | convolution fusion | flops 6445596672 | bytes 13631488 | tf_op jit(solution)/shard_map/rtd,rtf->df/dot_general | solution.py:691
  313.9 7.0 collective-permute-done.28
  326.7 16.0 %multiply_convert_fusion = (bf16[4,256,1536]{2,1,0:T(8,128)(2,1)}, bf16[4,256,1536]{2,1,0:T(8,128)(2,1)S(1)}) fusion(f32[4,256,1536]{2,1,0:T(8,128)} %fusion.11, f32[4,256,1536]{2,1,0:T(8,128)} %get-tuple-element.611, bf16[4,256,2048]{2,1,0:T(8,128)(2,1)S(1)} %copy-done.111, bf16[2048,1536]{1,0:T(8,128)(2,1)} %constant_dynamic-update-slice_fusion.3.refs_1_), kind=kOutput, calls=%fused_computation.22 | convolution fusion | flops 6478626816 | bytes 29360128 | tf_op jit(solution)/shard_map/rtd,df->rtf/dot_general | solution.py:683
  346.4 17.9 %back_project.5 = (f32[2,256,2048]{2,1,0:T(8,128)}, bf16[2,256,2048]{2,1,0:T(8,128)(2,1)}) custom-call(bf16[4,256,1536]{2,1,0:T(8,128)(2,1)S(1)} %get-tuple-element.272.refs_0_, bf16[4,256,1536]{2,1,0:T(8,128)(2,1)} %get-tuple-element.553.refs_1_, bf16[2048,1536]{1,0:T(8,128)(2,1)} %copy-done.81, bf16[2048,1536]{1,0:T(8,128)(2,1)} %get-tuple-element.256.refs_3_), custom_call_target="tpu_custom_call" | custom-call | flops 1 | bytes 1 | tf_op jit(solution)/shard_map/back_project/pallas_call | solution.py:585
  378.2 8.7 %bitcast_convert_fusion.1.refs_0_.refs_1_ = bf16[2048,1536]{1,0:T(8,128)(2,1)} fusion(bf16[4,256,2048]{2,1,0:T(8,128)(2,1)S(1)} %copy-done.83, bf16[4,256,1536]{2,1,0:T(8,128)(2,1)S(1)} %get-tuple-element.272.refs_0_), kind=kOutput, calls=%fused_computation.5 | convolution fusion | flops 6445596672 | bytes 13631488 | tf_op jit(solution)/shard_map/rtd,rtf->df/dot_general | solution.py:691
  395.0 6.9 collective-permute-done.35
  408.6 8.7 %bitcast_convert_fusion.refs_0_.refs_1_ = bf16[2048,1536]{1,0:T(8,128)(2,1)} fusion(bf16[4,256,2048]{2,1,0:T(8,128)(2,1)S(1)} %copy-done.84, bf16[4,256,1536]{2,1,0:T(8,128)(2,1)S(1)} %copy-done.87), kind=kOutput, calls=%fused_computation.4 | convolution fusion | flops 6445596672 | bytes 13631488 | tf_op jit(solution)/shard_map/rtd,rtf->df/dot_general | solution.py:691
  420.7 11.1 %back_project.6 = (f32[2,256,2048]{2,1,0:T(8,128)}, bf16[2,256,2048]{2,1,0:T(8,128)(2,1)}) custom-call(bf16[4,256,1536]{2,1,0:T(8,128)(2,1)S(1)} %copy-done.19, bf16[2048,1536]{1,0:T(8,128)(2,1)} %constant_dynamic-update-slice_fusion.3.refs_1_), custom_call_target="tpu_custom_call" | custom-call | flops 1 | bytes 1 | tf_op jit(solution)/shard_map/back_project/pallas_call | solution.py:585
  444.9 12.2 %backward_scan.1 = (bf16[4,256,640]{2,1,0:T(8,128)(2,1)S(1)}, f32[4,256,640]{2,1,0:T(8,128)S(1)}, f32[4,256,640]{2,1,0:T(8,128)}, f32[4,8,640]{2,1,0:T(8,128)S(1)}) custom-call(f32[4,256,640]{2,1,0:T(8,128)} %fusion.23.mixed_ref, f32[4,256,1280]{2,1,0:T(8,128)} %fusion.15.input_ref.pre_ref, f32[4,256,640]{2,1,0:T(8,128)} %get-tuple-element.552.state_ref, ...), custom_call_target="tpu_custom_call" | custom-call | flops 1 | bytes 1 | tf_op jit(solution)/shard_map/backward_scan/pallas_call | solution.py:519
  469.7 7.6 %all-to-all-done.1 = f32[8,8,640]{2,1,0:T(8,128)S(1)} async-done(((f32[8,8,640]{2,1,0:T(8,128)}), f32[8,8,640]{2,1,0:T(8,128)S(1)}, u32[]{:S(2)}, u32[]{:S(2)}) %all-to-all-start.1) | async-done | bytes 163872 | tf_op jit(solution)/shard_map/all_to_all | solution.py:243
  492.8 21.7 %branch_backward.1 = (bf16[4,256,1280]{2,1,0:T(8,128)(2,1)}, f32[4,8,640]{2,1,0:T(8,128)S(1)}, f32[4,8,640]{2,1,0:T(8,128)S(1)}, bf16[8,160,256]{2,1,0:T(8,128)(2,1)S(1)}, f32[8,640]{1,0:T(8,128)S(1)}) custom-call(f32[4,256,640]{2,1,0:T(8,128)} %copy-done.24, f32[4,256,640]{2,1,0:T(8,128)} %get-tuple-element.318.beta_ref, ...), custom_call_target="tpu_custom_call" | custom-call | flops 1 | bytes 1 | tf_op jit(solution)/shard_map/branch_backward/pallas_call | solution.py:545
  530.0 10.7 %back_project.7 = (f32[2,256,2048]{2,1,0:T(8,128)}, bf16[2,256,2048]{2,1,0:T(8,128)(2,1)}) custom-call(bf16[4,256,1280]{2,1,0:T(8,128)(2,1)S(1)} %fusion.31.refs_0_, bf16[2048,1280]{1,0:T(8,128)(2,1)} %copy-done.73), custom_call_target="tpu_custom_call" | custom-call | flops 1 | bytes 1 | tf_op jit(solution)/shard_map/back_project/pallas_call | solution.py:585
  559.1 9.3 %collective-permute-done.59.refs_2_ = bf16[256,1536]{1,0:T(8,128)(2,1)S(1)} collective-permute-done((bf16[256,1536]{1,0:T(8,128)(2,1)S(1)}, bf16[256,1536]{1,0:T(8,128)(2,1)S(1)}, u32[]{:S(2)}, u32[]{:S(2)}) %collective-permute-start.59) | collective-permute-done | bytes 786464 | tf_op jit(solution)/shard_map/ppermute | solution.py:125
  591.0 9.6 %collective-permute-done.61.refs_2_ = bf16[256,1536]{1,0:T(8,128)(2,1)S(1)} collective-permute-done((bf16[256,1536]{1,0:T(8,128)(2,1)}, bf16[256,1536]{1,0:T(8,128)(2,1)S(1)}, u32[]{:S(2)}, u32[]{:S(2)}) %collective-permute-start.61) | collective-permute-done | bytes 786464 | tf_op jit(solution)/shard_map/ppermute | solution.py:125
  646.2 7.0 collective-permute-done.67.refs_6_
  673.0 9.2 %shard_map.317 = f32[4,256,2048]{2,1,0:T(8,128)} custom-call(s32[4]{0:T(128)S(1)} %copy-done.69, s32[8]{0:T(128)S(1)} %copy-done.63, f32[4,256,2048]{2,1,0:T(8,128)} %base_ref.2, bf16[1,256,2048]{2,1,0:T(8,128)(2,1)} %subtract_convert_fusion.refs_0_, bf16[1,256,2048]{2,1,0:T(8,128)(2,1)} %collective-permute-done.66.refs_1_, ...), custom_call_target="tpu_custom_call" | custom-call | flops 1 | bytes 1 | tf_op jit(solution)/shard_map/pallas_call | solution.py:641
  682.2 8.2 %shard_map.318 = f32[4,256,2048]{2,1,0:T(8,128)} custom-call(s32[4]{0:T(128)S(1)} %copy-done.69, s32[8]{0:T(128)S(1)} %copy-done.63, f32[4,256,2048]{2,1,0:T(8,128)} %base_ref.3, bf16[1,256,2048]{2,1,0:T(8,128)(2,1)S(1)} %copy-done.17, bf16[1,256,2048]{2,1,0:T(8,128)(2,1)} %collective-permute-done.71.refs_1_, ...), custom_call_target="tpu_custom_call" | custom-call | flops 1 | bytes 1 | tf_op jit(solution)/shard_map/pallas_call | solution.py:641
  (573 shorter events, 378.9 us)
Async XLA Ops:
  31.9 28.4 %collective-permute-start.2 = (bf16[256,1920]{1,0:T(8,128)(2,1)}, bf16[256,1920]{1,0:T(8,128)(2,1)}, u32[]{:S(2)}, u32[]{:S(2)}) collective-permute-start(bf16[256,1920]{1,0:T(8,128)(2,1)} %collective-permute-done), channel_id=1, source_target_pairs={{0,8},{8,16},{16,24},{24,28},{28,20},{20,12},{12,4},{4,0},{1,9},{9... | collective-permute-start | bytes 2949128 | tf_op jit(solution)/shard_map/ppermute | solution.py:88
  33.4 26.9 %collective-permute-start.3 = (bf16[256,1920]{1,0:T(8,128)(2,1)}, bf16[256,1920]{1,0:T(8,128)(2,1)}, u32[]{:S(2)}, u32[]{:S(2)}) collective-permute-start(bf16[256,1920]{1,0:T(8,128)(2,1)} %collective-permute-done.1), channel_id=1, source_target_pairs={{8,0},{16,8},{24,16},{28,24},{20,28},{12,20},{4,12},{0,4},{9,1},{1... | collective-permute-start | bytes 2949128 | tf_op jit(solution)/shard_map/ppermute | solution.py:89
  97.6 31.4 %collective-permute-start.9 = (bf16[256,3072]{1,0:T(8,128)(2,1)}, bf16[256,3072]{1,0:T(8,128)(2,1)}, u32[]{:S(2)}, u32[]{:S(2)}) collective-permute-start(bf16[256,3072]{1,0:T(8,128)(2,1)} %pad_maximum_fusion.2), channel_id=1, source_target_pairs={{0,8},{8,16},{16,24},{24,28},{28,20},{20,12},{12,4},{4,0},{1,9},{9... | collective-permute-start | bytes 4718600 | tf_op jit(solution)/shard_map/ppermute | solution.py:88
  98.3 32.1 %collective-permute-start.10 = (bf16[256,3072]{1,0:T(8,128)(2,1)}, bf16[256,3072]{1,0:T(8,128)(2,1)}, u32[]{:S(2)}, u32[]{:S(2)}) collective-permute-start(bf16[256,3072]{1,0:T(8,128)(2,1)} %pad_maximum_fusion.2), channel_id=1, source_target_pairs={{8,0},{16,8},{24,16},{28,24},{20,28},{12,20},{4,12},{0,4},{9,1},{1... | collective-permute-start | bytes 4718600 | tf_op jit(solution)/shard_map/ppermute | solution.py:89
  165.1 37.1 %collective-permute-start.12 = (bf16[256,3072]{1,0:T(8,128)(2,1)}, bf16[256,3072]{1,0:T(8,128)(2,1)}, u32[]{:S(2)}, u32[]{:S(2)}) collective-permute-start(bf16[256,3072]{1,0:T(8,128)(2,1)} %collective-permute-done.9), channel_id=1, source_target_pairs={{0,8},{8,16},{16,24},{24,28},{28,20},{20,12},{12,4},{4,0},{1,9},{9... | collective-permute-start | bytes 4718600 | tf_op jit(solution)/shard_map/ppermute | solution.py:88
  165.1 37.1 %collective-permute-start.13 = (bf16[256,3072]{1,0:T(8,128)(2,1)}, bf16[256,3072]{1,0:T(8,128)(2,1)}, u32[]{:S(2)}, u32[]{:S(2)}) collective-permute-start(bf16[256,3072]{1,0:T(8,128)(2,1)} %collective-permute-done.10), channel_id=1, source_target_pairs={{8,0},{16,8},{24,16},{28,24},{20,28},{12,20},{4,12},{0,4},{9,1},{1... | collective-permute-start | bytes 4718600 | tf_op jit(solution)/shard_map/ppermute | solution.py:89
  172.2 34.7 %collective-permute-start.14 = (bf16[1,256,2048]{2,1,0:T(8,128)(2,1)S(1)}, bf16[1,256,2048]{2,1,0:T(8,128)(2,1)S(1)}, u32[]{:S(2)}, u32[]{:S(2)}) collective-permute-start(bf16[1,256,2048]{2,1,0:T(8,128)(2,1)S(1)} %slice.823), channel_id=1, source_target_pairs={{0,2},{1,3},{2,0},{3,1},{4,6},{5,7},{6,4},{7,5},{8,10},{9,11},{10,... | collective-permute-start | bytes 3145736 | tf_op jit(solution)/shard_map/ppermute | solution.py:209
  202.2 36.2 %collective-permute-start.15 = (bf16[256,3072]{1,0:T(8,128)(2,1)}, bf16[256,3072]{1,0:T(8,128)(2,1)S(1)}, u32[]{:S(2)}, u32[]{:S(2)}) collective-permute-start(bf16[256,3072]{1,0:T(8,128)(2,1)} %collective-permute-done.12), channel_id=1, source_target_pairs={{0,8},{8,16},{16,24},{24,28},{28,20},{20,12},{12,4},{4,0},{1,9},{9... | collective-permute-start | bytes 4718600 | tf_op jit(solution)/shard_map/ppermute | solution.py:88
  202.9 35.8 %collective-permute-start.16 = (bf16[256,3072]{1,0:T(8,128)(2,1)}, bf16[256,3072]{1,0:T(8,128)(2,1)S(1)}, u32[]{:S(2)}, u32[]{:S(2)}) collective-permute-start(bf16[256,3072]{1,0:T(8,128)(2,1)} %collective-permute-done.13), channel_id=1, source_target_pairs={{8,0},{16,8},{24,16},{28,24},{20,28},{12,20},{4,12},{0,4},{9,1},{1... | collective-permute-start | bytes 4718600 | tf_op jit(solution)/shard_map/ppermute | solution.py:89
  207.7 34.1 %collective-permute-start.23 = (bf16[1,256,2048]{2,1,0:T(8,128)(2,1)S(1)}, bf16[1,256,2048]{2,1,0:T(8,128)(2,1)S(1)}, u32[]{:S(2)}, u32[]{:S(2)}) collective-permute-start(bf16[1,256,2048]{2,1,0:T(8,128)(2,1)S(1)} %multiply_convert_fusion.2), channel_id=1, source_target_pairs={{0,2},{1,3},{2,0},{3,1},{4,6},{5,7},{6,4},{7,5},{8,10},{9,11},{10,... | collective-permute-start | bytes 3145736 | tf_op jit(solution)/shard_map/ppermute | solution.py:209
  212.8 47.9 %collective-permute-start.24 = (bf16[1,256,2048]{2,1,0:T(8,128)(2,1)S(1)}, bf16[1,256,2048]{2,1,0:T(8,128)(2,1)S(1)}, u32[]{:S(2)}, u32[]{:S(2)}) collective-permute-start(bf16[1,256,2048]{2,1,0:T(8,128)(2,1)S(1)} %multiply_convert_fusion.2), channel_id=1, source_target_pairs={{0,1},{1,0},{2,3},{3,2},{4,5},{5,4},{6,7},{7,6},{8,9},{9,8},{10,11... | collective-permute-start | bytes 3145736 | tf_op jit(solution)/shard_map/ppermute | solution.py:205
  406.7 26.8 %collective-permute-start.38 = (bf16[1,256,2048]{2,1,0:T(8,128)(2,1)}, bf16[1,256,2048]{2,1,0:T(8,128)(2,1)S(1)}, u32[]{:S(2)}, u32[]{:S(2)}) collective-permute-start(bf16[1,256,2048]{2,1,0:T(8,128)(2,1)} %get-tuple-element.543), channel_id=1, source_target_pairs={{0,2},{1,3},{2,0},{3,1},{4,6},{5,7},{6,4},{7,5},{8,10},{9,11},{10,... | collective-permute-start | bytes 3145736 | tf_op jit(solution)/shard_map/ppermute | solution.py:209
  434.0 43.6 %collective-permute-start.45 = (bf16[2,256,2048]{2,1,0:T(8,128)(2,1)}, bf16[2,256,2048]{2,1,0:T(8,128)(2,1)}, u32[]{:S(2)}, u32[]{:S(2)}) collective-permute-start(bf16[2,256,2048]{2,1,0:T(8,128)(2,1)} %get-tuple-element.309), channel_id=1, source_target_pairs={{0,1},{1,0},{2,3},{3,2},{4,5},{5,4},{6,7},{7,6},{8,9},{9,8},{10,11... | collective-permute-start | bytes 6291464 | tf_op jit(solution)/shard_map/ppermute | solution.py:205
  434.1 29.3 %collective-permute-start.46 = (bf16[256,1536]{1,0:T(8,128)(2,1)S(1)}, bf16[256,1536]{1,0:T(8,128)(2,1)S(1)}, u32[]{:S(2)}, u32[]{:S(2)}) collective-permute-start(bf16[256,1536]{1,0:T(8,128)(2,1)S(1)} %get-tuple-element.304), channel_id=1, source_target_pairs={{0,8},{8,16},{16,24},{24,28},{28,20},{20,12},{12,4},{4,0},{1,9},{9... | collective-permute-start | bytes 2359304 | tf_op jit(solution)/shard_map/ppermute | solution.py:125
  434.6 29.7 %collective-permute-start.47 = (bf16[256,1536]{1,0:T(8,128)(2,1)S(1)}, bf16[256,1536]{1,0:T(8,128)(2,1)S(1)}, u32[]{:S(2)}, u32[]{:S(2)}) collective-permute-start(bf16[256,1536]{1,0:T(8,128)(2,1)S(1)} %get-tuple-element.305), channel_id=1, source_target_pairs={{8,0},{16,8},{24,16},{28,24},{20,28},{12,20},{4,12},{0,4},{9,1},{1... | collective-permute-start | bytes 2359304 | tf_op jit(solution)/shard_map/ppermute | solution.py:125
  436.1 26.3 %collective-permute-start.48 = (bf16[128,1536]{1,0:T(8,128)(2,1)S(1)}, bf16[128,1536]{1,0:T(8,128)(2,1)S(1)}, u32[]{:S(2)}, u32[]{:S(2)}) collective-permute-start(bf16[128,1536]{1,0:T(8,128)(2,1)S(1)} %get-tuple-element.302), channel_id=1, source_target_pairs={{0,8},{8,16},{16,24},{24,28},{28,20},{20,12},{12,4},{4,0},{1,9},{9... | collective-permute-start | bytes 1179656 | tf_op jit(solution)/shard_map/ppermute | solution.py:125
  483.4 31.2 %collective-permute-start.50 = (bf16[1,256,2048]{2,1,0:T(8,128)(2,1)S(1)}, bf16[1,256,2048]{2,1,0:T(8,128)(2,1)S(1)}, u32[]{:S(2)}, u32[]{:S(2)}) collective-permute-start(bf16[1,256,2048]{2,1,0:T(8,128)(2,1)S(1)} %slice.821), channel_id=1, source_target_pairs={{0,2},{1,3},{2,0},{3,1},{4,6},{5,7},{6,4},{7,5},{8,10},{9,11},{10,... | collective-permute-start | bytes 3145736 | tf_op jit(solution)/shard_map/ppermute | solution.py:209
  486.7 27.9 %collective-permute-start.51 = (bf16[256,1536]{1,0:T(8,128)(2,1)S(1)}, bf16[256,1536]{1,0:T(8,128)(2,1)S(1)}, u32[]{:S(2)}, u32[]{:S(2)}) collective-permute-start(bf16[256,1536]{1,0:T(8,128)(2,1)S(1)} %get-tuple-element.328), channel_id=1, source_target_pairs={{0,8},{8,16},{16,24},{24,28},{28,20},{20,12},{12,4},{4,0},{1,9},{9... | collective-permute-start | bytes 2359304 | tf_op jit(solution)/shard_map/ppermute | solution.py:125
  486.7 27.9 %collective-permute-start.52 = (bf16[256,1536]{1,0:T(8,128)(2,1)S(1)}, bf16[256,1536]{1,0:T(8,128)(2,1)S(1)}, u32[]{:S(2)}, u32[]{:S(2)}) collective-permute-start(bf16[256,1536]{1,0:T(8,128)(2,1)S(1)} %get-tuple-element.329), channel_id=1, source_target_pairs={{8,0},{16,8},{24,16},{28,24},{20,28},{12,20},{4,12},{0,4},{9,1},{1... | collective-permute-start | bytes 2359304 | tf_op jit(solution)/shard_map/ppermute | solution.py:125
  490.3 51.8 %collective-permute-start.54 = (bf16[256,1536]{1,0:T(8,128)(2,1)S(1)}, bf16[256,1536]{1,0:T(8,128)(2,1)S(1)}, u32[]{:S(2)}, u32[]{:S(2)}) collective-permute-start(bf16[256,1536]{1,0:T(8,128)(2,1)S(1)} %get-tuple-element.345), channel_id=1, source_target_pairs={{0,8},{8,16},{16,24},{24,28},{28,20},{20,12},{12,4},{4,0},{1,9},{9... | collective-permute-start | bytes 2359304 | tf_op jit(solution)/shard_map/ppermute | solution.py:125
  490.4 51.7 %collective-permute-start.55 = (bf16[256,1536]{1,0:T(8,128)(2,1)S(1)}, bf16[256,1536]{1,0:T(8,128)(2,1)S(1)}, u32[]{:S(2)}, u32[]{:S(2)}) collective-permute-start(bf16[256,1536]{1,0:T(8,128)(2,1)S(1)} %get-tuple-element.346), channel_id=1, source_target_pairs={{8,0},{16,8},{24,16},{28,24},{20,28},{12,20},{4,12},{0,4},{9,1},{1... | collective-permute-start | bytes 2359304 | tf_op jit(solution)/shard_map/ppermute | solution.py:125
  570.9 37.5 %collective-permute-start.63 = (bf16[1,256,2048]{2,1,0:T(8,128)(2,1)}, bf16[1,256,2048]{2,1,0:T(8,128)(2,1)}, u32[]{:S(2)}, u32[]{:S(2)}) collective-permute-start(bf16[1,256,2048]{2,1,0:T(8,128)(2,1)} %slice.820), channel_id=1, source_target_pairs={{0,2},{1,3},{2,0},{3,1},{4,6},{5,7},{6,4},{7,5},{8,10},{9,11},{10,... | collective-permute-start | bytes 3145736 | tf_op jit(solution)/shard_map/ppermute | solution.py:209
  574.5 83.6 %collective-permute-start.71 = (bf16[1,256,2048]{2,1,0:T(8,128)(2,1)}, bf16[1,256,2048]{2,1,0:T(8,128)(2,1)}, u32[]{:S(2)}, u32[]{:S(2)}) collective-permute-start(bf16[1,256,2048]{2,1,0:T(8,128)(2,1)} %get-tuple-element.556.refs_0_), channel_id=1, source_target_pairs={{0,2},{1,3},{2,0},{3,1},{4,6},{5,7},{6,4},{7,5},{8,10},{9,11},{10,... | collective-permute-start | bytes 3145736 | tf_op jit(solution)/shard_map/ppermute | solution.py:209
  586.8 44.0 %all-to-all-start.2 = ((bf16[8,163,256]{2,1,0:T(8,128)(2,1)}), bf16[8,163,256]{2,1,0:T(8,128)(2,1)}, u32[]{:S(2)}, u32[]{:S(2)}) async-start(bf16[8,163,256]{2,1,0:T(8,128)(2,1)} %reshape.193), calls=%async_computation.2 | async-start | bytes 1376256 | tf_op jit(solution)/shard_map/all_to_all | solution.py:903
  623.4 40.5 %collective-permute-start.69 = (bf16[1,256,2048]{2,1,0:T(8,128)(2,1)}, bf16[1,256,2048]{2,1,0:T(8,128)(2,1)}, u32[]{:S(2)}, u32[]{:S(2)}) collective-permute-start(bf16[1,256,2048]{2,1,0:T(8,128)(2,1)} %subtract_convert_fusion.refs_0_), channel_id=1, source_target_pairs={{0,1},{1,0},{2,3},{3,2},{4,5},{5,4},{6,7},{7,6},{8,9},{9,8},{10,11... | collective-permute-start | bytes 3145736 | tf_op jit(solution)/shard_map/ppermute | solution.py:205
  626.4 26.8 %collective-permute-start.67 = (bf16[256,1920]{1,0:T(8,128)(2,1)}, bf16[256,1920]{1,0:T(8,128)(2,1)S(1)}, u32[]{:S(2)}, u32[]{:S(2)}) collective-permute-start(bf16[256,1920]{1,0:T(8,128)(2,1)} %get-tuple-element.385), channel_id=1, source_target_pairs={{0,8},{8,16},{16,24},{24,28},{28,20},{20,12},{12,4},{4,0},{1,9},{9... | collective-permute-start | bytes 2949128 | tf_op jit(solution)/shard_map/ppermute | solution.py:125
  630.8 25.9 %collective-permute-start.68 = (bf16[256,1920]{1,0:T(8,128)(2,1)}, bf16[256,1920]{1,0:T(8,128)(2,1)S(1)}, u32[]{:S(2)}, u32[]{:S(2)}) collective-permute-start(bf16[256,1920]{1,0:T(8,128)(2,1)} %get-tuple-element.386), channel_id=1, source_target_pairs={{8,0},{16,8},{24,16},{28,24},{20,28},{12,20},{4,12},{0,4},{9,1},{1... | collective-permute-start | bytes 2949128 | tf_op jit(solution)/shard_map/ppermute | solution.py:125
  631.7 35.0 %all-to-all-start.4 = ((f32[32,16,256]{2,1,0:T(8,128)}), f32[32,16,256]{2,1,0:T(8,128)}, u32[]{:S(2)}, u32[]{:S(2)}) async-start(f32[32,16,256]{2,1,0:T(8,128)} %broadcast_in_dim.83), calls=%async_computation.4 | async-start | bytes 1048576 | tf_op jit(solution)/shard_map/all_to_all | solution.py:243
  663.5 27.0 %collective-permute-start.74 = (bf16[256,1920]{1,0:T(8,128)(2,1)}, bf16[256,1920]{1,0:T(8,128)(2,1)}, u32[]{:S(2)}, u32[]{:S(2)}) collective-permute-start(bf16[256,1920]{1,0:T(8,128)(2,1)} %get-tuple-element.389), channel_id=1, source_target_pairs={{0,8},{8,16},{16,24},{24,28},{28,20},{20,12},{12,4},{4,0},{1,9},{9... | collective-permute-start | bytes 2949128 | tf_op jit(solution)/shard_map/ppermute | solution.py:125
  663.9 26.5 %collective-permute-start.75 = (bf16[256,1920]{1,0:T(8,128)(2,1)}, bf16[256,1920]{1,0:T(8,128)(2,1)}, u32[]{:S(2)}, u32[]{:S(2)}) collective-permute-start(bf16[256,1920]{1,0:T(8,128)(2,1)} %get-tuple-element.390), channel_id=1, source_target_pairs={{8,0},{16,8},{24,16},{28,24},{20,28},{12,20},{4,12},{0,4},{9,1},{1... | collective-permute-start | bytes 2949128 | tf_op jit(solution)/shard_map/ppermute | solution.py:125
  667.7 35.4 %all-to-all-start.3 = ((bf16[8,163,256]{2,1,0:T(8,128)(2,1)}), bf16[8,163,256]{2,1,0:T(8,128)(2,1)}, u32[]{:S(2)}, u32[]{:S(2)}) async-start(bf16[8,163,256]{2,1,0:T(8,128)(2,1)} %broadcast_in_dim.82), calls=%async_computation.3 | async-start | bytes 1376256 | tf_op jit(solution)/shard_map/all_to_all | solution.py:243
  696.0 25.9 %collective-permute-start.77 = (bf16[256,1920]{1,0:T(8,128)(2,1)}, bf16[256,1920]{1,0:T(8,128)(2,1)}, u32[]{:S(2)}, u32[]{:S(2)}) collective-permute-start(bf16[256,1920]{1,0:T(8,128)(2,1)} %get-tuple-element.404), channel_id=1, source_target_pairs={{8,0},{16,8},{24,16},{28,24},{20,28},{12,20},{4,12},{0,4},{9,1},{1... | collective-permute-start | bytes 2949128 | tf_op jit(solution)/shard_map/ppermute | solution.py:125
  (166 other events, 2758.2 us)

commit v3 on v2

--- a/solution.py
+++ b/solution.py
@@ -775,7 +775,7 @@
     came = gather_one.step()
     hidden_one = relative_norm(tokens, norm1_gain, first_maps)
     hidden_before = relative_norm(before, norm1_gain, first_maps)
-    recur_weights = after_that(recur_gate_w, (came, hidden_before))
+    recur_weights = after_that(recur_gate_w, (came, hidden_one))
     came = gather_one.step()
     high, low = gate_matrix(recur_weights, input_gate_w)
     gather_two = Gather(mlp_shards, gather_one.step())
@@ -860,22 +860,18 @@
     )
     export = meet(export, reduce_gate, reduce_up)
     incoming = carried(export, True)[:, None, :]
-    result_kept, result_beyond = joined(result_kept, after_that(result_came, export))
-    incoming = after_that(incoming, result_beyond)
     reduce_gate.others = reduce_up.others = incoming
     sent = (reduce_up.step(), reduce_gate.step())
-    result_arrived = to_far(after_that(result_beyond, incoming))
     grad_pre, tail, head, gate_grads, sums = run_backward(
         tail_decay, grad_part, incoming, state, carry, recur, gate, conv, pre, halo, masks,
         conv_weight, coef, high, low, grad_pre_gate,
     )
-    head = meet(after_that(head, result_arrived), reduce_up)
+    head = meet(head, reduce_up)
     sent = reduce_up.step()
+    result_kept, result_beyond = joined(result_kept, after_that(result_came, (head, sent)))
+    result_arrived = to_far(result_beyond)
     beyond = lax.ppermute(head, "seq", [(s + 1, s) for s in range(seq_count - 1)])
-    result_delta = after + (result_kept + after_that(result_arrived, (sent, head)).astype(F32))
-    result_delta = (result_delta - tokens_own).astype(LOW)
-    result_far, result_near = to_far(result_delta), to_near(result_delta)
-    out_part = outer_sum(grad_one, after_that(mixed, result_delta))
+    out_part = outer_sum(grad_one, after_that(mixed, result_beyond))
     beyond = after_that(beyond, out_part)
     grad_pre = lax.dynamic_update_slice(grad_pre, (tail + beyond).astype(LOW), (0, length - 8, 0))
     kept, away = back_project([grad_pre], [in_gate])
@@ -899,7 +895,10 @@
         ]
     )
     small = after_that(small.reshape(seq_count, -1, WINDOW), in_part)
-    in_part = after_that(in_part, small)
+    result_arrived = after_that(result_arrived, in_part)
+    result_delta = (after + (result_kept + result_arrived.astype(F32)) - tokens_own).astype(LOW)
+    result_far, result_near = to_far(result_delta), to_near(result_delta)
+    in_part = after_that(in_part, (small, result_delta))
     small = lax.all_to_all(small, "seq", 0, 0, tiled=True)
     small = jnp.sum(small.astype(F32), axis=0).astype(LOW)
     every = to_all(small, "seq")
@@ -924,7 +923,7 @@
     late_maps = after_that(maps, (sent, far))
     token_grad = assemble(cotangent, [own, far, near, to_near(far)], late_maps)
     result_pieces = [
-        result_delta, result_far, result_near, to_near(after_that(result_far, beyond)),
+        result_delta, result_far, result_near, to_near(after_that(result_far, far)),
     ]
     late_maps = after_that(maps, token_grad)
     result = assemble(tokens, result_pieces, late_maps)

time: 737 us -> 733 us (level)
  waiting for transfers between devices: 201 us -> 187 us
    ppermute x16, waiting for transfers between devices: 40.5 us -> 27.9 us  [step(): lax.ppermute(up, 'seq', ahead)]
    unnamed x270 -> x266, local copies, waits for them, and re-layouts: 72.9 us -> 73.6 us
  transfers between devices with their start and end apart: 83 -> 83, of which waited for: 38 -> 37; matrix products, arithmetic and copies ran while one was open for 29% -> 31% of each run, Pallas kernels for 22% -> 22%
where the time goes in v3:
time: 733 us; the launch traced here: 722 us
  waiting for transfers between devices  187 us (26%)
  Pallas kernels  169 us (23%)
  local copies, waits for them, and re-layouts  110 us (15%)
  starting transfers between devices  101 us (14%)
  matrix products  91.5 us (12%)
  other arithmetic  60.8 us (8%)
    ppermute x12, waiting for transfers between devices, step(): self.up.append(lax.ppermute(first, 'seq', ahead))  103 us
    unnamed x266, local copies, waits for them, and re-layouts  73.6 us
    dot_general x6, matrix products, project(): return jnp.einsum('rtd,df->rtf', left, right, preferred_element_type=F32)  48.3 us
    pallas_call x4, Pallas kernels, back_project(): pl.pallas_call(kernel, grid=(width // tile,), in_specs=in_specs, out_spec...  46.1 us
    dot_general x6, matrix products, outer_sum(): jnp.einsum('rtd,rtf->df', left, right, preferred_element_type=F32)  43.1 us
    pallas_call x20, Pallas kernels, ring_step(): pl.pallas_call(kernel, grid=(grid,), in_specs=blocks + got_specs, out_spe...  40.9 us
    pallas_call x6, Pallas kernels, arranged(): pl.pallas_call(kernel, grid_spec=pltpu.PrefetchScalarGridSpec(num_scalar_...  33 us
    ppermute x16, waiting for transfers between devices, step(): lax.ppermute(up, 'seq', ahead)  27.9 us
  transfers between devices with their start and end apart: 83, of which 37 were waited for; matrix products, arithmetic and copies ran while one was open for 31% of the time, Pallas kernels for 22%

profile of v3, /device:TPU:0, one launch (start us, length us, event | category | flops | bytes accessed | tf_op | source)
XLA Modules:
  0.0 722.0 jit_solution(6569112941216747549)
XLA Ops:
  22.5 7.9 %collective-permute-done = bf16[256,1920]{1,0:T(8,128)(2,1)} collective-permute-done((bf16[256,1920]{1,0:T(8,128)(2,1)}, bf16[256,1920]{1,0:T(8,128)(2,1)}, u32[]{:S(2)}, u32[]{:S(2)}) %collective-permute-start) | collective-permute-done | bytes 983072 | tf_op jit(solution)/shard_map/ppermute | solution.py:88
  41.3 5.3 shard_map.313
  47.8 11.4 %collective-permute-done.8.values_ref = f32[4,8,2048]{2,1,0:T(8,128)S(1)} collective-permute-done((f32[4,8,2048]{2,1,0:T(8,128)S(1)}, f32[4,8,2048]{2,1,0:T(8,128)S(1)}, u32[]{:S(2)}, u32[]{:S(2)}) %collective-permute-start.8) | collective-permute-done | bytes 262176 | tf_op jit(solution)/shard_map/ppermute | solution.py:773
  68.0 14.6 %collective-permute-done.4 = bf16[256,1920]{1,0:T(8,128)(2,1)} collective-permute-done((bf16[256,1920]{1,0:T(8,128)(2,1)}, bf16[256,1920]{1,0:T(8,128)(2,1)}, u32[]{:S(2)}, u32[]{:S(2)}) %collective-permute-start.4) | collective-permute-done | bytes 983072 | tf_op jit(solution)/shard_map/ppermute | solution.py:88
  100.6 7.3 %fusion.15.input_ref.pre_ref = f32[4,256,1280]{2,1,0:T(8,128)} fusion(bf16[4,256,2048]{2,1,0:T(8,128)(2,1)S(1)} %shard_map.313, bf16[2048,1280]{1,0:T(8,128)(2,1)S(1)} %slice_dynamic-update-slice_fusion.28.refs_1_), kind=kOutput, calls=%fused_computation.30 | convolution fusion | flops 5368709120 | bytes 14680064 | tf_op jit(solution)/shard_map/rtd,df->rtf/dot_general | solution.py:683
  108.0 14.9 %forward_scan.1 = (f32[4,256,640]{2,1,0:T(8,128)S(1)}, f32[4,256,640]{2,1,0:T(8,128)}, f32[4,256,640]{2,1,0:T(8,128)}, f32[4,256,640]{2,1,0:T(8,128)}, f32[4,256,640]{2,1,0:T(8,128)}, /*index=5*/f32[4,8,640]{2,1,0:T(8,128)S(1)}) custom-call(f32[4,256,1280]{2,1,0:T(8,128)} %fusion.15.input_ref.pre_ref, f32[4,8,1280]{2,1,0:T(8,128)S(1)} %fusion.13.halo_ref, ...), custom_call_target="tpu_custom_call" | custom-call | flops 1 | bytes 1 | tf_op jit(solution)/shard_map/forward_scan/pallas_call | solution.py:500
  137.0 5.6 all-to-all-done
  143.5 5.9 fusion.22
  149.4 6.4 back_project.4
  179.0 6.9 shard_map.315
  185.9 16.3 %collective-permute-done.12 = bf16[256,3072]{1,0:T(8,128)(2,1)} collective-permute-done((bf16[256,3072]{1,0:T(8,128)(2,1)}, bf16[256,3072]{1,0:T(8,128)(2,1)}, u32[]{:S(2)}, u32[]{:S(2)}) %collective-permute-start.12) | collective-permute-done | bytes 1572896 | tf_op jit(solution)/shard_map/ppermute | solution.py:88
  213.1 25.4 %collective-permute-done.15 = bf16[256,3072]{1,0:T(8,128)(2,1)S(1)} collective-permute-done((bf16[256,3072]{1,0:T(8,128)(2,1)}, bf16[256,3072]{1,0:T(8,128)(2,1)S(1)}, u32[]{:S(2)}, u32[]{:S(2)}) %collective-permute-start.15) | collective-permute-done | bytes 1572896 | tf_op jit(solution)/shard_map/ppermute | solution.py:88
  242.9 14.0 %collective-permute-done.17 = bf16[128,3072]{1,0:T(8,128)(2,1)S(1)} collective-permute-done((bf16[128,3072]{1,0:T(8,128)(2,1)S(1)}, bf16[128,3072]{1,0:T(8,128)(2,1)S(1)}, u32[]{:S(2)}, u32[]{:S(2)}) %collective-permute-start.17) | collective-permute-done | bytes 786464 | tf_op jit(solution)/shard_map/ppermute | solution.py:88
  260.7 8.6 %fusion.11 = f32[4,256,1536]{2,1,0:T(8,128)} fusion(bf16[2048,1536]{1,0:T(8,128)(2,1)S(1)} %get-tuple-element.565.refs_2_, bf16[1,256,2048]{2,1,0:T(8,128)(2,1)S(1)} %collective-permute-done.25, bf16[1,256,2048]{2,1,0:T(8,128)(2,1)S(1)} %collective-permute-done.24, bf16[1,256,2048]{2,1,0:T(8,128)(2,1)S(1)} %collective-permute-done.23, ...), kind=kOutput, calls=%fused_computation.20 | convolution fusion | flops 6448742400 | bytes 16777216 | tf_op jit(solution)/shard_map/rtd,df->rtf/dot_general | solution.py:683
  269.3 5.4 collective-permute-done.19
  276.8 10.5 %multiply_convert_fusion.1 = (bf16[4,256,1536]{2,1,0:T(8,128)(2,1)S(1)}, f32[4,256,1536]{2,1,0:T(8,128)}) fusion(f32[4,256,1536]{2,1,0:T(8,128)} %fusion.11, bf16[2048,1536]{1,0:T(8,128)(2,1)S(1)} %copy-done.79, bf16[1,256,2048]{2,1,0:T(8,128)(2,1)S(1)} %collective-permute-done.25, bf16[1,256,2048]{2,1,0:T(8,128)(2,1)S(1)} %collective-permute-done.24, ...), kind=kOutput, calls=%fused_computation.23 | convolution fusion | flops 6464471040 | bytes 26214400 | tf_op jit(solution)/shard_map/rtd,df->rtf/dot_general | solution.py:683
  294.6 11.1 %bitcast_convert_fusion.2.refs_0_.refs_1_ = bf16[2048,1536]{1,0:T(8,128)(2,1)} fusion(bf16[4,256,2048]{2,1,0:T(8,128)(2,1)} %get-tuple-element.254, bf16[4,256,1536]{2,1,0:T(8,128)(2,1)S(1)} %get-tuple-element.295.refs_0_), kind=kOutput, calls=%fused_computation.6 | convolution fusion | flops 6445596672 | bytes 13631488 | tf_op jit(solution)/shard_map/rtd,rtf->df/dot_general | solution.py:691
  313.8 6.9 collective-permute-done.28
  326.9 16.0 %multiply_convert_fusion = (bf16[4,256,1536]{2,1,0:T(8,128)(2,1)}, bf16[4,256,1536]{2,1,0:T(8,128)(2,1)S(1)}) fusion(f32[4,256,1536]{2,1,0:T(8,128)} %fusion.11, f32[4,256,1536]{2,1,0:T(8,128)} %get-tuple-element.605, bf16[4,256,2048]{2,1,0:T(8,128)(2,1)S(1)} %copy-done.109, bf16[2048,1536]{1,0:T(8,128)(2,1)} %constant_dynamic-update-slice_fusion.3.refs_1_), kind=kOutput, calls=%fused_computation.22 | convolution fusion | flops 6478626816 | bytes 29360128 | tf_op jit(solution)/shard_map/rtd,df->rtf/dot_general | solution.py:683
  346.6 17.9 %back_project.5 = (f32[2,256,2048]{2,1,0:T(8,128)}, bf16[2,256,2048]{2,1,0:T(8,128)(2,1)S(1)}) custom-call(bf16[4,256,1536]{2,1,0:T(8,128)(2,1)S(1)} %get-tuple-element.269.refs_0_, bf16[4,256,1536]{2,1,0:T(8,128)(2,1)} %get-tuple-element.547.refs_1_, bf16[2048,1536]{1,0:T(8,128)(2,1)} %copy-done.78, bf16[2048,1536]{1,0:T(8,128)(2,1)} %get-tuple-element.253.refs_3_), custom_call_target="tpu_custom_call" | custom-call | flops 1 | bytes 1 | tf_op jit(solution)/shard_map/back_project/pallas_call | solution.py:585
  378.7 8.7 %bitcast_convert_fusion.1.refs_0_.refs_1_ = bf16[2048,1536]{1,0:T(8,128)(2,1)} fusion(bf16[4,256,2048]{2,1,0:T(8,128)(2,1)S(1)} %copy-done.80, bf16[4,256,1536]{2,1,0:T(8,128)(2,1)S(1)} %get-tuple-element.269.refs_0_), kind=kOutput, calls=%fused_computation.5 | convolution fusion | flops 6445596672 | bytes 13631488 | tf_op jit(solution)/shard_map/rtd,rtf->df/dot_general | solution.py:691
  395.2 7.3 %collective-permute-done.35 = bf16[1,256,2048]{2,1,0:T(8,128)(2,1)} collective-permute-done((bf16[1,256,2048]{2,1,0:T(8,128)(2,1)}, bf16[1,256,2048]{2,1,0:T(8,128)(2,1)}, u32[]{:S(2)}, u32[]{:S(2)}) %collective-permute-start.35) | collective-permute-done | bytes 1048608 | tf_op jit(solution)/shard_map/ppermute | solution.py:209
  410.7 8.8 %bitcast_convert_fusion.refs_0_.refs_1_ = bf16[2048,1536]{1,0:T(8,128)(2,1)} fusion(bf16[4,256,2048]{2,1,0:T(8,128)(2,1)S(1)} %copy-done.81, bf16[4,256,1536]{2,1,0:T(8,128)(2,1)S(1)} %copy-done.87), kind=kOutput, calls=%fused_computation.4 | convolution fusion | flops 6445596672 | bytes 13631488 | tf_op jit(solution)/shard_map/rtd,rtf->df/dot_general | solution.py:691
  424.6 11.0 %back_project.6 = (f32[2,256,2048]{2,1,0:T(8,128)}, bf16[2,256,2048]{2,1,0:T(8,128)(2,1)}) custom-call(bf16[4,256,1536]{2,1,0:T(8,128)(2,1)S(1)} %copy-done.17, bf16[2048,1536]{1,0:T(8,128)(2,1)} %constant_dynamic-update-slice_fusion.3.refs_1_), custom_call_target="tpu_custom_call" | custom-call | flops 1 | bytes 1 | tf_op jit(solution)/shard_map/back_project/pallas_call | solution.py:585
  449.4 12.2 %backward_scan.1 = (bf16[4,256,640]{2,1,0:T(8,128)(2,1)S(1)}, f32[4,256,640]{2,1,0:T(8,128)S(1)}, f32[4,256,640]{2,1,0:T(8,128)}, f32[4,8,640]{2,1,0:T(8,128)S(1)}) custom-call(f32[4,256,640]{2,1,0:T(8,128)} %fusion.23.mixed_ref, f32[4,256,1280]{2,1,0:T(8,128)} %fusion.15.input_ref.pre_ref, f32[4,256,640]{2,1,0:T(8,128)} %get-tuple-element.546.state_ref, ...), custom_call_target="tpu_custom_call" | custom-call | flops 1 | bytes 1 | tf_op jit(solution)/shard_map/backward_scan/pallas_call | solution.py:519
  489.9 21.9 %branch_backward.1 = (bf16[4,256,1280]{2,1,0:T(8,128)(2,1)}, f32[4,8,640]{2,1,0:T(8,128)S(1)}, f32[4,8,640]{2,1,0:T(8,128)S(1)}, bf16[8,160,256]{2,1,0:T(8,128)(2,1)S(1)}, f32[8,640]{1,0:T(8,128)S(1)}) custom-call(f32[4,256,640]{2,1,0:T(8,128)} %copy-done.22, f32[4,256,640]{2,1,0:T(8,128)} %get-tuple-element.310.beta_ref, ...), custom_call_target="tpu_custom_call" | custom-call | flops 1 | bytes 1 | tf_op jit(solution)/shard_map/branch_backward/pallas_call | solution.py:545
  529.8 10.8 %back_project.7 = (f32[2,256,2048]{2,1,0:T(8,128)}, bf16[2,256,2048]{2,1,0:T(8,128)(2,1)}) custom-call(bf16[4,256,1280]{2,1,0:T(8,128)(2,1)S(1)} %fusion.31.refs_0_, bf16[2048,1280]{1,0:T(8,128)(2,1)} %copy-done.69), custom_call_target="tpu_custom_call" | custom-call | flops 1 | bytes 1 | tf_op jit(solution)/shard_map/back_project/pallas_call | solution.py:585
  567.4 5.7 collective-permute-done.58.refs_2_
  589.7 5.8 collective-permute-done.61.refs_2_
  637.1 9.0 %collective-permute-done.66.refs_1_ = bf16[1,256,2048]{2,1,0:T(8,128)(2,1)} collective-permute-done((bf16[1,256,2048]{2,1,0:T(8,128)(2,1)}, bf16[1,256,2048]{2,1,0:T(8,128)(2,1)}, u32[]{:S(2)}, u32[]{:S(2)}) %collective-permute-start.66) | collective-permute-done | bytes 1048608 | tf_op jit(solution)/shard_map/ppermute | solution.py:209
  668.7 8.8 %shard_map.317 = f32[4,256,2048]{2,1,0:T(8,128)} custom-call(s32[4]{0:T(128)S(1)} %copy-done.64, s32[8]{0:T(128)S(1)} %copy-done.58, f32[4,256,2048]{2,1,0:T(8,128)} %base_ref.2, bf16[1,256,2048]{2,1,0:T(8,128)(2,1)} %subtract_convert_fusion.refs_0_, bf16[1,256,2048]{2,1,0:T(8,128)(2,1)} %collective-permute-done.66.refs_1_, ...), custom_call_target="tpu_custom_call" | custom-call | flops 1 | bytes 1 | tf_op jit(solution)/shard_map/pallas_call | solution.py:641
  677.6 8.5 %shard_map.318 = f32[4,256,2048]{2,1,0:T(8,128)} custom-call(s32[4]{0:T(128)S(1)} %copy-done.64, s32[8]{0:T(128)S(1)} %copy-done.58, f32[4,256,2048]{2,1,0:T(8,128)} %base_ref.3, bf16[1,256,2048]{2,1,0:T(8,128)(2,1)} %get-tuple-element.550.refs_0_, bf16[1,256,2048]{2,1,0:T(8,128)(2,1)} %collective-permute-done.71.refs_1_, ...), custom_call_target="tpu_custom_call" | custom-call | flops 1 | bytes 1 | tf_op jit(solution)/shard_map/pallas_call | solution.py:641
  (569 shorter events, 382.2 us)
Async XLA Ops:
  31.9 28.4 %collective-permute-start.2 = (bf16[256,1920]{1,0:T(8,128)(2,1)}, bf16[256,1920]{1,0:T(8,128)(2,1)}, u32[]{:S(2)}, u32[]{:S(2)}) collective-permute-start(bf16[256,1920]{1,0:T(8,128)(2,1)} %collective-permute-done), channel_id=1, source_target_pairs={{0,8},{8,16},{16,24},{24,28},{28,20},{20,12},{12,4},{4,0},{1,9},{9... | collective-permute-start | bytes 2949128 | tf_op jit(solution)/shard_map/ppermute | solution.py:88
  33.4 26.9 %collective-permute-start.3 = (bf16[256,1920]{1,0:T(8,128)(2,1)}, bf16[256,1920]{1,0:T(8,128)(2,1)}, u32[]{:S(2)}, u32[]{:S(2)}) collective-permute-start(bf16[256,1920]{1,0:T(8,128)(2,1)} %collective-permute-done.1), channel_id=1, source_target_pairs={{8,0},{16,8},{24,16},{28,24},{20,28},{12,20},{4,12},{0,4},{9,1},{1... | collective-permute-start | bytes 2949128 | tf_op jit(solution)/shard_map/ppermute | solution.py:89
  97.6 31.4 %collective-permute-start.9 = (bf16[256,3072]{1,0:T(8,128)(2,1)}, bf16[256,3072]{1,0:T(8,128)(2,1)}, u32[]{:S(2)}, u32[]{:S(2)}) collective-permute-start(bf16[256,3072]{1,0:T(8,128)(2,1)} %pad_maximum_fusion.2), channel_id=1, source_target_pairs={{0,8},{8,16},{16,24},{24,28},{28,20},{20,12},{12,4},{4,0},{1,9},{9... | collective-permute-start | bytes 4718600 | tf_op jit(solution)/shard_map/ppermute | solution.py:88
  98.3 32.1 %collective-permute-start.10 = (bf16[256,3072]{1,0:T(8,128)(2,1)}, bf16[256,3072]{1,0:T(8,128)(2,1)}, u32[]{:S(2)}, u32[]{:S(2)}) collective-permute-start(bf16[256,3072]{1,0:T(8,128)(2,1)} %pad_maximum_fusion.2), channel_id=1, source_target_pairs={{8,0},{16,8},{24,16},{28,24},{20,28},{12,20},{4,12},{0,4},{9,1},{1... | collective-permute-start | bytes 4718600 | tf_op jit(solution)/shard_map/ppermute | solution.py:89
  165.1 37.1 %collective-permute-start.12 = (bf16[256,3072]{1,0:T(8,128)(2,1)}, bf16[256,3072]{1,0:T(8,128)(2,1)}, u32[]{:S(2)}, u32[]{:S(2)}) collective-permute-start(bf16[256,3072]{1,0:T(8,128)(2,1)} %collective-permute-done.9), channel_id=1, source_target_pairs={{0,8},{8,16},{16,24},{24,28},{28,20},{20,12},{12,4},{4,0},{1,9},{9... | collective-permute-start | bytes 4718600 | tf_op jit(solution)/shard_map/ppermute | solution.py:88
  165.1 37.1 %collective-permute-start.13 = (bf16[256,3072]{1,0:T(8,128)(2,1)}, bf16[256,3072]{1,0:T(8,128)(2,1)}, u32[]{:S(2)}, u32[]{:S(2)}) collective-permute-start(bf16[256,3072]{1,0:T(8,128)(2,1)} %collective-permute-done.10), channel_id=1, source_target_pairs={{8,0},{16,8},{24,16},{28,24},{20,28},{12,20},{4,12},{0,4},{9,1},{1... | collective-permute-start | bytes 4718600 | tf_op jit(solution)/shard_map/ppermute | solution.py:89
  172.4 34.5 %collective-permute-start.14 = (bf16[1,256,2048]{2,1,0:T(8,128)(2,1)S(1)}, bf16[1,256,2048]{2,1,0:T(8,128)(2,1)}, u32[]{:S(2)}, u32[]{:S(2)}) collective-permute-start(bf16[1,256,2048]{2,1,0:T(8,128)(2,1)S(1)} %slice.823), channel_id=1, source_target_pairs={{0,2},{1,3},{2,0},{3,1},{4,6},{5,7},{6,4},{7,5},{8,10},{9,11},{10,... | collective-permute-start | bytes 3145736 | tf_op jit(solution)/shard_map/ppermute | solution.py:209
  202.2 36.2 %collective-permute-start.15 = (bf16[256,3072]{1,0:T(8,128)(2,1)}, bf16[256,3072]{1,0:T(8,128)(2,1)S(1)}, u32[]{:S(2)}, u32[]{:S(2)}) collective-permute-start(bf16[256,3072]{1,0:T(8,128)(2,1)} %collective-permute-done.12), channel_id=1, source_target_pairs={{0,8},{8,16},{16,24},{24,28},{28,20},{20,12},{12,4},{4,0},{1,9},{9... | collective-permute-start | bytes 4718600 | tf_op jit(solution)/shard_map/ppermute | solution.py:88
  202.9 35.8 %collective-permute-start.16 = (bf16[256,3072]{1,0:T(8,128)(2,1)}, bf16[256,3072]{1,0:T(8,128)(2,1)S(1)}, u32[]{:S(2)}, u32[]{:S(2)}) collective-permute-start(bf16[256,3072]{1,0:T(8,128)(2,1)} %collective-permute-done.13), channel_id=1, source_target_pairs={{8,0},{16,8},{24,16},{28,24},{20,28},{12,20},{4,12},{0,4},{9,1},{1... | collective-permute-start | bytes 4718600 | tf_op jit(solution)/shard_map/ppermute | solution.py:89
  209.0 32.8 %collective-permute-start.23 = (bf16[1,256,2048]{2,1,0:T(8,128)(2,1)S(1)}, bf16[1,256,2048]{2,1,0:T(8,128)(2,1)S(1)}, u32[]{:S(2)}, u32[]{:S(2)}) collective-permute-start(bf16[1,256,2048]{2,1,0:T(8,128)(2,1)S(1)} %multiply_convert_fusion.2), channel_id=1, source_target_pairs={{0,2},{1,3},{2,0},{3,1},{4,6},{5,7},{6,4},{7,5},{8,10},{9,11},{10,... | collective-permute-start | bytes 3145736 | tf_op jit(solution)/shard_map/ppermute | solution.py:209
  213.1 47.6 %collective-permute-start.24 = (bf16[1,256,2048]{2,1,0:T(8,128)(2,1)S(1)}, bf16[1,256,2048]{2,1,0:T(8,128)(2,1)S(1)}, u32[]{:S(2)}, u32[]{:S(2)}) collective-permute-start(bf16[1,256,2048]{2,1,0:T(8,128)(2,1)S(1)} %multiply_convert_fusion.2), channel_id=1, source_target_pairs={{0,1},{1,0},{2,3},{3,2},{4,5},{5,4},{6,7},{7,6},{8,9},{9,8},{10,11... | collective-permute-start | bytes 3145736 | tf_op jit(solution)/shard_map/ppermute | solution.py:205
  393.1 26.3 %collective-permute-start.39 = (bf16[256,1536]{1,0:T(8,128)(2,1)S(1)}, bf16[256,1536]{1,0:T(8,128)(2,1)S(1)}, u32[]{:S(2)}, u32[]{:S(2)}) collective-permute-start(bf16[256,1536]{1,0:T(8,128)(2,1)S(1)} %get-tuple-element.281), channel_id=1, source_target_pairs={{0,8},{8,16},{16,24},{24,28},{28,20},{20,12},{12,4},{4,0},{1,9},{9... | collective-permute-start | bytes 2359304 | tf_op jit(solution)/shard_map/ppermute | solution.py:125
  409.2 28.2 %collective-permute-start.38 = (bf16[1,256,2048]{2,1,0:T(8,128)(2,1)S(1)}, bf16[1,256,2048]{2,1,0:T(8,128)(2,1)S(1)}, u32[]{:S(2)}, u32[]{:S(2)}) collective-permute-start(bf16[1,256,2048]{2,1,0:T(8,128)(2,1)S(1)} %get-tuple-element.537), channel_id=1, source_target_pairs={{0,2},{1,3},{2,0},{3,1},{4,6},{5,7},{6,4},{7,5},{8,10},{9,11},{10,... | collective-permute-start | bytes 3145736 | tf_op jit(solution)/shard_map/ppermute | solution.py:209
  438.0 29.4 %collective-permute-start.46 = (bf16[256,1536]{1,0:T(8,128)(2,1)S(1)}, bf16[256,1536]{1,0:T(8,128)(2,1)S(1)}, u32[]{:S(2)}, u32[]{:S(2)}) collective-permute-start(bf16[256,1536]{1,0:T(8,128)(2,1)S(1)} %get-tuple-element.301), channel_id=1, source_target_pairs={{0,8},{8,16},{16,24},{24,28},{28,20},{20,12},{12,4},{4,0},{1,9},{9... | collective-permute-start | bytes 2359304 | tf_op jit(solution)/shard_map/ppermute | solution.py:125
  438.4 30.0 %collective-permute-start.47 = (bf16[256,1536]{1,0:T(8,128)(2,1)S(1)}, bf16[256,1536]{1,0:T(8,128)(2,1)S(1)}, u32[]{:S(2)}, u32[]{:S(2)}) collective-permute-start(bf16[256,1536]{1,0:T(8,128)(2,1)S(1)} %get-tuple-element.302), channel_id=1, source_target_pairs={{8,0},{16,8},{24,16},{28,24},{20,28},{12,20},{4,12},{0,4},{9,1},{1... | collective-permute-start | bytes 2359304 | tf_op jit(solution)/shard_map/ppermute | solution.py:125
  442.2 75.4 %collective-permute-start.45 = (bf16[2,256,2048]{2,1,0:T(8,128)(2,1)}, bf16[2,256,2048]{2,1,0:T(8,128)(2,1)}, u32[]{:S(2)}, u32[]{:S(2)}) collective-permute-start(bf16[2,256,2048]{2,1,0:T(8,128)(2,1)} %get-tuple-element.306), channel_id=1, source_target_pairs={{0,1},{1,0},{2,3},{3,2},{4,5},{5,4},{6,7},{7,6},{8,9},{9,8},{10,11... | collective-permute-start | bytes 6291464 | tf_op jit(solution)/shard_map/ppermute | solution.py:205
  484.1 27.7 %collective-permute-start.50 = (bf16[256,1536]{1,0:T(8,128)(2,1)}, bf16[256,1536]{1,0:T(8,128)(2,1)S(1)}, u32[]{:S(2)}, u32[]{:S(2)}) collective-permute-start(bf16[256,1536]{1,0:T(8,128)(2,1)} %copy-done.66), channel_id=1, source_target_pairs={{0,8},{8,16},{16,24},{24,28},{28,20},{20,12},{12,4},{4,0},{1,9},{9... | collective-permute-start | bytes 2359304 | tf_op jit(solution)/shard_map/ppermute | solution.py:125
  484.2 27.6 %collective-permute-start.51 = (bf16[256,1536]{1,0:T(8,128)(2,1)}, bf16[256,1536]{1,0:T(8,128)(2,1)S(1)}, u32[]{:S(2)}, u32[]{:S(2)}) collective-permute-start(bf16[256,1536]{1,0:T(8,128)(2,1)} %copy-done.65), channel_id=1, source_target_pairs={{8,0},{16,8},{24,16},{28,24},{20,28},{12,20},{4,12},{0,4},{9,1},{1... | collective-permute-start | bytes 2359304 | tf_op jit(solution)/shard_map/ppermute | solution.py:125
  487.8 54.2 %collective-permute-start.53 = (bf16[256,1536]{1,0:T(8,128)(2,1)S(1)}, bf16[256,1536]{1,0:T(8,128)(2,1)S(1)}, u32[]{:S(2)}, u32[]{:S(2)}) collective-permute-start(bf16[256,1536]{1,0:T(8,128)(2,1)S(1)} %get-tuple-element.338), channel_id=1, source_target_pairs={{0,8},{8,16},{16,24},{24,28},{28,20},{20,12},{12,4},{4,0},{1,9},{9... | collective-permute-start | bytes 2359304 | tf_op jit(solution)/shard_map/ppermute | solution.py:125
  487.9 54.1 %collective-permute-start.54 = (bf16[256,1536]{1,0:T(8,128)(2,1)S(1)}, bf16[256,1536]{1,0:T(8,128)(2,1)S(1)}, u32[]{:S(2)}, u32[]{:S(2)}) collective-permute-start(bf16[256,1536]{1,0:T(8,128)(2,1)S(1)} %get-tuple-element.339), channel_id=1, source_target_pairs={{8,0},{16,8},{24,16},{28,24},{20,28},{12,20},{4,12},{0,4},{9,1},{1... | collective-permute-start | bytes 2359304 | tf_op jit(solution)/shard_map/ppermute | solution.py:125
  515.2 27.7 %collective-permute-start.55 = (bf16[256,1536]{1,0:T(8,128)(2,1)S(1)}, bf16[256,1536]{1,0:T(8,128)(2,1)S(1)}, u32[]{:S(2)}, u32[]{:S(2)}) collective-permute-start(bf16[256,1536]{1,0:T(8,128)(2,1)S(1)} %get-tuple-element.326), channel_id=1, source_target_pairs={{0,8},{8,16},{16,24},{24,28},{28,20},{20,12},{12,4},{4,0},{1,9},{9... | collective-permute-start | bytes 2359304 | tf_op jit(solution)/shard_map/ppermute | solution.py:125
  549.5 33.5 %collective-permute-start.60 = (bf16[1,256,2048]{2,1,0:T(8,128)(2,1)}, bf16[1,256,2048]{2,1,0:T(8,128)(2,1)S(1)}, u32[]{:S(2)}, u32[]{:S(2)}) collective-permute-start(bf16[1,256,2048]{2,1,0:T(8,128)(2,1)} %slice.821), channel_id=1, source_target_pairs={{0,2},{1,3},{2,0},{3,1},{4,6},{5,7},{6,4},{7,5},{8,10},{9,11},{10,... | collective-permute-start | bytes 3145736 | tf_op jit(solution)/shard_map/ppermute | solution.py:209
  576.7 26.4 %collective-permute-start.63 = (bf16[1,256,2048]{2,1,0:T(8,128)(2,1)}, bf16[1,256,2048]{2,1,0:T(8,128)(2,1)}, u32[]{:S(2)}, u32[]{:S(2)}) collective-permute-start(bf16[1,256,2048]{2,1,0:T(8,128)(2,1)} %slice.820), channel_id=1, source_target_pairs={{0,2},{1,3},{2,0},{3,1},{4,6},{5,7},{6,4},{7,5},{8,10},{9,11},{10,... | collective-permute-start | bytes 3145736 | tf_op jit(solution)/shard_map/ppermute | solution.py:209
  584.9 69.3 %collective-permute-start.71 = (bf16[1,256,2048]{2,1,0:T(8,128)(2,1)}, bf16[1,256,2048]{2,1,0:T(8,128)(2,1)}, u32[]{:S(2)}, u32[]{:S(2)}) collective-permute-start(bf16[1,256,2048]{2,1,0:T(8,128)(2,1)} %get-tuple-element.550.refs_0_), channel_id=1, source_target_pairs={{0,2},{1,3},{2,0},{3,1},{4,6},{5,7},{6,4},{7,5},{8,10},{9,11},{10,... | collective-permute-start | bytes 3145736 | tf_op jit(solution)/shard_map/ppermute | solution.py:209
  585.5 41.6 %all-to-all-start.2 = ((bf16[8,163,256]{2,1,0:T(8,128)(2,1)}), bf16[8,163,256]{2,1,0:T(8,128)(2,1)}, u32[]{:S(2)}, u32[]{:S(2)}) async-start(bf16[8,163,256]{2,1,0:T(8,128)(2,1)} %reshape.193), calls=%async_computation.2 | async-start | bytes 1376256 | tf_op jit(solution)/shard_map/all_to_all | solution.py:902
  617.0 29.1 %collective-permute-start.66 = (bf16[1,256,2048]{2,1,0:T(8,128)(2,1)}, bf16[1,256,2048]{2,1,0:T(8,128)(2,1)}, u32[]{:S(2)}, u32[]{:S(2)}) collective-permute-start(bf16[1,256,2048]{2,1,0:T(8,128)(2,1)} %subtract_convert_fusion.refs_0_), channel_id=1, source_target_pairs={{0,2},{1,3},{2,0},{3,1},{4,6},{5,7},{6,4},{7,5},{8,10},{9,11},{10,... | collective-permute-start | bytes 3145736 | tf_op jit(solution)/shard_map/ppermute | solution.py:209
  618.8 41.0 %collective-permute-start.69 = (bf16[1,256,2048]{2,1,0:T(8,128)(2,1)}, bf16[1,256,2048]{2,1,0:T(8,128)(2,1)}, u32[]{:S(2)}, u32[]{:S(2)}) collective-permute-start(bf16[1,256,2048]{2,1,0:T(8,128)(2,1)} %subtract_convert_fusion.refs_0_), channel_id=1, source_target_pairs={{0,1},{1,0},{2,3},{3,2},{4,5},{5,4},{6,7},{7,6},{8,9},{9,8},{10,11... | collective-permute-start | bytes 3145736 | tf_op jit(solution)/shard_map/ppermute | solution.py:205
  621.8 27.5 %collective-permute-start.67 = (bf16[256,1920]{1,0:T(8,128)(2,1)}, bf16[256,1920]{1,0:T(8,128)(2,1)S(1)}, u32[]{:S(2)}, u32[]{:S(2)}) collective-permute-start(bf16[256,1920]{1,0:T(8,128)(2,1)} %get-tuple-element.379), channel_id=1, source_target_pairs={{0,8},{8,16},{16,24},{24,28},{28,20},{20,12},{12,4},{4,0},{1,9},{9... | collective-permute-start | bytes 2949128 | tf_op jit(solution)/shard_map/ppermute | solution.py:125
  627.9 34.7 %all-to-all-start.4 = ((f32[32,16,256]{2,1,0:T(8,128)}), f32[32,16,256]{2,1,0:T(8,128)}, u32[]{:S(2)}, u32[]{:S(2)}) async-start(f32[32,16,256]{2,1,0:T(8,128)} %broadcast_in_dim.83), calls=%async_computation.4 | async-start | bytes 1048576 | tf_op jit(solution)/shard_map/all_to_all | solution.py:243
  659.4 26.7 %collective-permute-start.74 = (bf16[256,1920]{1,0:T(8,128)(2,1)}, bf16[256,1920]{1,0:T(8,128)(2,1)}, u32[]{:S(2)}, u32[]{:S(2)}) collective-permute-start(bf16[256,1920]{1,0:T(8,128)(2,1)} %get-tuple-element.383), channel_id=1, source_target_pairs={{0,8},{8,16},{16,24},{24,28},{28,20},{20,12},{12,4},{4,0},{1,9},{9... | collective-permute-start | bytes 2949128 | tf_op jit(solution)/shard_map/ppermute | solution.py:125
  659.7 26.4 %collective-permute-start.75 = (bf16[256,1920]{1,0:T(8,128)(2,1)}, bf16[256,1920]{1,0:T(8,128)(2,1)}, u32[]{:S(2)}, u32[]{:S(2)}) collective-permute-start(bf16[256,1920]{1,0:T(8,128)(2,1)} %get-tuple-element.384), channel_id=1, source_target_pairs={{8,0},{16,8},{24,16},{28,24},{20,28},{12,20},{4,12},{0,4},{9,1},{1... | collective-permute-start | bytes 2949128 | tf_op jit(solution)/shard_map/ppermute | solution.py:125
  663.6 35.3 %all-to-all-start.3 = ((bf16[8,163,256]{2,1,0:T(8,128)(2,1)}), bf16[8,163,256]{2,1,0:T(8,128)(2,1)}, u32[]{:S(2)}, u32[]{:S(2)}) async-start(bf16[8,163,256]{2,1,0:T(8,128)(2,1)} %broadcast_in_dim.82), calls=%async_computation.3 | async-start | bytes 1376256 | tf_op jit(solution)/shard_map/all_to_all | solution.py:243
  (164 other events, 3350.9 us)
